TPU v7x, 32 devices: a whole 2x2x4 slice. The times are simulated.
32 devices in a mesh: section: 4 (over y, x), fsdp: 8 (over z, core).
Axes of the slice: x: 2, y: 2, z: 4, core: 2. Of those that a mesh axis runs over, the one named last changes fastest.
Arguments:
- saved_inputs: bfloat16 [4, 2, 2048, 2048], P('section', None, 'fsdp'), may hold values from -600 to 600
- saved_queries: bfloat16 [4, 2, 2048, 1024], P('section', None, 'fsdp'), may hold values from -300 to 300
- saved_keys: bfloat16 [4, 2, 2048, 256], P('section', None, 'fsdp'), may hold values from -6 to 6
- saved_values: bfloat16 [4, 2, 2048, 256], P('section', None, 'fsdp'), may hold values from -6 to 6
- cotangent: bfloat16 [2, 2048, 2048], P(None, 'fsdp'), may hold values from -6 to 6
- norm_gain: bfloat16 [4, 2048], P('section'), may hold values from 0.099609375 to 1.8984375
- query_weight: bfloat16 [4, 2048, 1024], P('section', 'fsdp'), may hold values from -0.125 to 0.125
- key_weight: bfloat16 [4, 2048, 256], P('section', 'fsdp'), may hold values from -0.125 to 0.125
- value_weight: bfloat16 [4, 2048, 256], P('section', 'fsdp'), may hold values from -0.125 to 0.125
- output_weight: bfloat16 [4, 2048, 1024], P('section', 'fsdp'), may hold values from -0.1875 to 0.1875
Outputs:
- act_grads: bfloat16 [4, 2, 2048, 2048], P('section', None, 'fsdp')
- grad_query: bfloat16 [4, 2048, 1024], P('section', 'fsdp')
- grad_key: bfloat16 [4, 2048, 256], P('section', 'fsdp')
- grad_value: bfloat16 [4, 2048, 256], P('section', 'fsdp')
- grad_output: bfloat16 [4, 2048, 1024], P('section', 'fsdp')
All inputs are finite; a program needn't handle non-finite values.
Results may differ from a plain program's by a relative error of at most 0.024.
Values may be sent and summed in bfloat16 or wider, within the bound.
A program may use at most 128 MiB of HBM per device.

v0:
```python
import math

import jax
import jax.numpy as jnp
from jax import lax
from jax.sharding import PartitionSpec as P

HEADS = 16
KVH = 4
HD = 64


norm_eps = 1e-05
rotary_base = 500000.0
masked_score = -1e30


def passed_along(block, axis, distance):
    devices = range(lax.axis_size(axis))
    route = [(i - distance, i) for i in devices if i - distance in devices]
    return lax.ppermute(block, axis, route)


def rotary_tables(length, head_size):
    half_size = head_size // 2
    inverse = jnp.exp(
        -(2.0 * jnp.arange(half_size, dtype=jnp.float32) / head_size) * math.log(rotary_base)
    )
    angles = jnp.arange(length, dtype=jnp.float32)[:, None] * inverse[None, :]
    return (jnp.cos(angles), jnp.sin(angles))


def rotate_back(grad_rows, cosine_table, sine_table):
    half_size = grad_rows.shape[-1] // 2
    front_half = grad_rows[..., :half_size]
    back_half = grad_rows[..., half_size:]
    cos_rows = cosine_table[:, None, :]
    sin_rows = sine_table[:, None, :]
    return jnp.concatenate(
        [
            front_half * cos_rows + back_half * sin_rows,
            back_half * cos_rows - front_half * sin_rows,
        ],
        axis=-1,
    )


def norm_parts(inputs):
    inputs_f = inputs.astype(jnp.float32)
    scale_inv = lax.rsqrt(jnp.mean(inputs_f * inputs_f, axis=-1, keepdims=True) + norm_eps)
    return (inputs_f * scale_inv, scale_inv)


def forward_parts(inputs, queries, keys, values, gain_row):
    length = inputs.shape[0]
    groups = HEADS // KVH
    unit_rows, scale_inv = norm_parts(inputs)
    normed = (unit_rows * gain_row.astype(jnp.float32)).astype(jnp.bfloat16)
    query_grid = queries.reshape(length, KVH, groups, HD)
    key_grid = keys.reshape(length, KVH, HD)
    value_grid = values.reshape(length, KVH, HD)
    scores = jnp.einsum(
        "tkgd,skd->kgts", query_grid, key_grid, preferred_element_type=jnp.float32
    ) * (1.0 / math.sqrt(HD))
    causal = jnp.arange(length)[:, None] >= jnp.arange(length)[None, :]
    scores = jnp.where(causal, scores, masked_score)
    row_peak = jnp.max(scores, axis=-1, keepdims=True)
    weights = jnp.exp(scores - row_peak)
    attn_probs = (weights / jnp.sum(weights, axis=-1, keepdims=True)).astype(jnp.bfloat16)
    attn_out = jnp.einsum(
        "kgts,skd->tkgd", attn_probs, value_grid, preferred_element_type=jnp.float32
    )
    return (attn_probs, normed, attn_out.astype(jnp.bfloat16).reshape(length, -1))


def backward_step(
    inputs,
    queries,
    keys,
    values,
    attn_probs,
    upstream,
    gain_row,
    out_full,
    in_full,
    cosine_table,
    sine_table,
):
    length = inputs.shape[0]
    groups = HEADS // KVH
    scaling = 1.0 / math.sqrt(HD)
    unit_rows, scale_inv = norm_parts(inputs)
    d_attn = jnp.dot(upstream, out_full, preferred_element_type=jnp.float32).astype(jnp.bfloat16)
    attn_grid = d_attn.reshape(length, KVH, groups, HD)
    query_grid = queries.reshape(length, KVH, groups, HD)
    key_grid = keys.reshape(length, KVH, HD)
    value_grid = values.reshape(length, KVH, HD)
    d_probs = jnp.einsum(
        "tkgd,skd->kgts", attn_grid, value_grid, preferred_element_type=jnp.float32
    )
    probs_f = attn_probs.astype(jnp.float32)
    row_inner = jnp.sum(probs_f * d_probs, axis=-1, keepdims=True)
    d_scores = (probs_f * (d_probs - row_inner) * scaling).astype(jnp.bfloat16)
    d_query = jnp.einsum("kgts,skd->tkgd", d_scores, key_grid, preferred_element_type=jnp.float32)
    d_key = jnp.einsum("kgts,tkgd->skd", d_scores, query_grid, preferred_element_type=jnp.float32)
    d_value = jnp.einsum(
        "kgts,tkgd->skd", attn_probs, attn_grid, preferred_element_type=jnp.float32
    )
    d_query = rotate_back(d_query.reshape(length, HEADS, HD), cosine_table, sine_table).reshape(
        length, -1
    )
    d_key = rotate_back(d_key, cosine_table, sine_table).reshape(length, -1)
    grad_qkv = jnp.concatenate([d_query, d_key, d_value.reshape(length, -1)], axis=1).astype(
        jnp.bfloat16
    )
    d_normed = lax.dot_general(
        grad_qkv, in_full, (((1,), (1,)), ((), ())), preferred_element_type=jnp.float32
    )
    scaled = d_normed * gain_row.astype(jnp.float32)
    d_inputs = scale_inv * (
        scaled - unit_rows * jnp.mean(scaled * unit_rows, axis=-1, keepdims=True)
    )
    grad_in = (upstream.astype(jnp.float32) + d_inputs).astype(jnp.bfloat16)
    return (grad_in, grad_qkv)


def select_micro(stacked, micro_index):
    return lax.dynamic_index_in_dim(stacked, micro_index, 0, keepdims=False)


def on_device(
    saved_inputs,
    saved_queries,
    saved_keys,
    saved_values,
    cotangent,
    norm_gain,
    query_weight,
    key_weight,
    value_weight,
    output_weight,
):
    sections = lax.axis_size("section")
    section_index = lax.axis_index("section")
    last_section = sections - 1
    inputs = saved_inputs[0]
    queries = saved_queries[0]
    keys_all = saved_keys[0]
    values_all = saved_values[0]
    gain_row = norm_gain[0]
    micro_count = inputs.shape[0]
    length = inputs.shape[1]
    width = inputs.shape[2]
    cosine_table, sine_table = rotary_tables(length, HD)
    forward_all = jax.vmap(forward_parts, in_axes=(0, 0, 0, 0, None))
    query_full, key_full, value_full, output_full = (
        lax.all_gather(query_weight, "fsdp", axis=1, tiled=True),
        lax.all_gather(key_weight, "fsdp", axis=1, tiled=True),
        lax.all_gather(value_weight, "fsdp", axis=1, tiled=True),
        lax.all_gather(output_weight, "fsdp", axis=1, tiled=True),
    )
    attn_probs, normed, attn_out = forward_all(inputs, queries, keys_all, values_all, gain_row)
    in_full = jnp.concatenate([query_full[0], key_full[0], value_full[0]], axis=1)
    out_full = output_full[0]
    qkv_width = in_full.shape[1]

    def one_micro(micro_index, upstream):
        return backward_step(
            select_micro(inputs, micro_index),
            select_micro(queries, micro_index),
            select_micro(keys_all, micro_index),
            select_micro(values_all, micro_index),
            select_micro(attn_probs, micro_index),
            upstream,
            gain_row,
            out_full,
            in_full,
            cosine_table,
            sine_table,
        )

    grads_zero = jnp.zeros((micro_count, length, width), jnp.bfloat16)
    qkv_zero = jnp.zeros((micro_count, length, qkv_width), jnp.bfloat16)

    def turn(turn_index, state_in):
        arrived, grads_store, qkv_store, upstream_store = state_in
        active = turn_index == last_section - section_index
        upstream_all = jnp.where(section_index == last_section, cotangent, arrived)

        def run_section(rows_in):
            results = [
                one_micro(micro_index, rows_in[micro_index]) for micro_index in range(micro_count)
            ]
            return (
                jnp.stack([result[0] for result in results]),
                jnp.stack([result[1] for result in results]),
            )

        def skip_section(rows_in):
            return (grads_zero, qkv_zero)

        grad_all, qkv_all = lax.cond(active, run_section, skip_section, upstream_all)
        grads_store = jnp.where(active, grad_all, grads_store)
        qkv_store = jnp.where(active, qkv_all, qkv_store)
        upstream_store = jnp.where(active, upstream_all, upstream_store)
        arrived = passed_along(grad_all, "section", -1)
        return (arrived, grads_store, qkv_store, upstream_store)

    initial = (grads_zero, grads_zero, qkv_zero, grads_zero)
    leftover, grads_store, qkv_store, upstream_store = lax.fori_loop(0, sections, turn, initial)
    normed_flat = normed.reshape(micro_count * length, width)
    qkv_flat = qkv_store.reshape(micro_count * length, qkv_width)
    attn_flat = attn_out.reshape(micro_count * length, -1)
    upstream_flat = upstream_store.reshape(micro_count * length, width)
    summed = lax.psum_scatter(
        jnp.concatenate(
            [
                lax.dot_general(
                    normed_flat,
                    qkv_flat,
                    (((0,), (0,)), ((), ())),
                    preferred_element_type=jnp.float32,
                ),
                lax.dot_general(
                    upstream_flat,
                    attn_flat,
                    (((0,), (0,)), ((), ())),
                    preferred_element_type=jnp.float32,
                ),
            ],
            axis=1,
        ).astype(jnp.bfloat16),
        "fsdp",
        scatter_dimension=0,
        tiled=True,
    )
    query_cols = query_weight.shape[2]
    key_cols = key_weight.shape[2]
    grad_query = summed[:, :query_cols]
    grad_key = summed[:, query_cols : query_cols + key_cols]
    grad_value = summed[:, query_cols + key_cols : qkv_width]
    grad_output = summed[:, qkv_width:]
    return (
        grads_store[None],
        grad_query[None],
        grad_key[None],
        grad_value[None],
        grad_output[None],
    )


def solution(mesh):
    return jax.shard_map(
        on_device,
        mesh=mesh,
        in_specs=(
            P("section", None, "fsdp", None),
            P("section", None, "fsdp", None),
            P("section", None, "fsdp", None),
            P("section", None, "fsdp", None),
            P(None, "fsdp", None),
            P("section", None),
            P("section", "fsdp", None),
            P("section", "fsdp", None),
            P("section", "fsdp", None),
            P("section", "fsdp", None),
        ),
        out_specs=(
            P("section", None, "fsdp", None),
            P("section", "fsdp", None),
            P("section", "fsdp", None),
            P("section", "fsdp", None),
            P("section", "fsdp", None),
        ),
        check_vma=False,
    )
```

profile of v0, /device:TPU:0, one launch (start us, length us, event | category | flops | bytes accessed | tf_op | source)
XLA Modules:
  0.0 766.8 jit_solution(5658243010568604388)
XLA Ops:
  11.4 1.1 copy.44
  12.5 1.2 copy.46
  14.2 4.9 fusion.118
  19.2 4.5 divide_convert_fusion
  25.6 1.1 copy.51
  26.7 1.3 copy.75
  29.1 5.3 all-gather.9.cloned.1.call-done
  34.5 23.3 %all-gather.11.cloned.1.call-done = bf16[1,2048,256]{2,1,0:T(8,128)(2,1)} async-done(((bf16[1,256,256]{2,1,0:T(8,128)(2,1)}), bf16[1,2048,256]{2,1,0:T(8,128)(2,1)}) %all-gather.11.cloned.1.call-update) | async-done | bytes 1048592 | tf_op jit(solution)/shard_map/all_gather | solution.py:159
  57.8 48.4 %all-gather.7.cloned.1.call-done = bf16[1,2048,1024]{2,1,0:T(8,128)(2,1)} async-done(((bf16[1,256,1024]{2,1,0:T(8,128)(2,1)}), bf16[1,2048,1024]{2,1,0:T(8,128)(2,1)}) %all-gather.7.cloned.1.call-update) | async-done | bytes 4194320 | tf_op jit(solution)/shard_map/all_gather | solution.py:157
  106.2 7.9 %pad_maximum_fusion.2 = bf16[2048,1536]{1,0:T(8,128)(2,1)} fusion(bf16[2048,256]{1,0:T(8,128)(2,1)} %bitcast.342, bf16[2048,256]{1,0:T(8,128)(2,1)} %bitcast.341, bf16[2048,1024]{1,0:T(8,128)(2,1)} %bitcast.333), kind=kLoop, calls=%fused_computation.124 | loop fusion | flops 18874368 | bytes 12582912 | tf_op jit(solution)/shard_map/concatenate | solution.py:163
  114.1 39.4 %all-gather.5.cloned.1.call-done = bf16[1,2048,1024]{2,1,0:T(8,128)(2,1)} async-done(((bf16[1,256,1024]{2,1,0:T(8,128)(2,1)}), bf16[1,2048,1024]{2,1,0:T(8,128)(2,1)}) %all-gather.5.cloned.1.call-update) | async-done | bytes 4194320 | tf_op jit(solution)/shard_map/all_gather | solution.py:160
  153.6 1.6 broadcast_in_dim.28
  155.2 471.7 %while.25 = (s32[]{:T(128)}, bf16[2,256,2048]{2,1,0:T(8,128)(2,1)}, bf16[2,256,2048]{2,1,0:T(8,128)(2,1)}, bf16[2,256,1536]{1,2,0:T(8,128)(2,1)}, bf16[2,256,204...) while((s32[]{:T(128)}, bf16[2,256,2048]{2,1,0:T(8,128)(2,1)}, ...), condition=%wide.region_11.12_spmd.clone.clone.clone.clone, body=%wide.region_2.11_spmd.clone.clone.clone.clone.sunk | while | flops 6516534272 | bytes 260389968 | solution.py:210
  155.3 3.7 select_select_fusion.6
  159.0 2.9 conditional.6
  159.0 1.3 broadcast_in_dim.5
  160.3 1.6 broadcast_in_dim.4
  161.9 1.3 collective-permute-start
  163.2 1.6 select_select_fusion.7
  165.7 46.1 %collective-permute-done = bf16[2,256,2048]{2,1,0:T(8,128)(2,1)} collective-permute-done((bf16[2,256,2048]{2,1,0:T(8,128)(2,1)}, bf16[2,256,2048]{2,1,0:T(8,128)(2,1)}, u32[]{:S(2)}, u32[]{:S(2)}) %collective-permute-start) | collective-permute-done | bytes 2097184 | tf_op jit(solution)/shard_map/while/body/eval_jaxpr/ppermute | solution.py:21
  212.0 4.3 select_select_fusion.6
  216.3 2.9 conditional.6
  216.3 1.3 broadcast_in_dim.5
  217.6 1.6 broadcast_in_dim.4
  219.2 1.3 collective-permute-start
  220.5 3.3 select_select_fusion.7
  224.4 44.6 %collective-permute-done = bf16[2,256,2048]{2,1,0:T(8,128)(2,1)} collective-permute-done((bf16[2,256,2048]{2,1,0:T(8,128)(2,1)}, bf16[2,256,2048]{2,1,0:T(8,128)(2,1)}, u32[]{:S(2)}, u32[]{:S(2)}) %collective-permute-start) | collective-permute-done | bytes 2097184 | tf_op jit(solution)/shard_map/while/body/eval_jaxpr/ppermute | solution.py:21
  269.1 4.3 select_select_fusion.6
  273.5 2.9 conditional.6
  273.5 1.3 broadcast_in_dim.5
  274.7 1.6 broadcast_in_dim.4
  276.3 1.3 collective-permute-start
  277.6 3.3 select_select_fusion.7
  281.5 227.6 %collective-permute-done = bf16[2,256,2048]{2,1,0:T(8,128)(2,1)} collective-permute-done((bf16[2,256,2048]{2,1,0:T(8,128)(2,1)}, bf16[2,256,2048]{2,1,0:T(8,128)(2,1)}, u32[]{:S(2)}, u32[]{:S(2)}) %collective-permute-start) | collective-permute-done | bytes 2097184 | tf_op jit(solution)/shard_map/while/body/eval_jaxpr/ppermute | solution.py:21
  509.3 4.3 select_select_fusion.6
  513.6 64.8 %conditional.6 = (bf16[2,256,2048]{2,1,0:T(8,128)(2,1)}, bf16[2,256,1536]{1,2,0:T(8,128)(2,1)}) conditional(s32[]{:T(128)} %convert_element_type.207, () %tuple.112, (bf16[2,256,2048]{2,1,0:T(8,128)(2,1)S(1)}, bf16[2,256,2048]{2,1,0:T(8,128)(2,1)S(1)}, bf16[2,4,4,256,256]{3,4,2,1,0:T(8,128)(2,1)}, bf16[2048,1024]{1,0:T(8,128)(2,1)S(1)}, ...), branch_computations={%region_3.3_spmd, %region_4.10_spmd.clone} | conditional | flops 6509710336 | bytes 189577616 | solution.py:202
  514.3 2.0 fusion.116
  517.1 2.1 convolution_convert_fusion
  519.2 2.1 convolution_convert_fusion.1
  521.3 1.2 copy.73
  522.5 1.2 copy.74
  523.8 3.0 fusion.66
  526.8 3.1 fusion.69
  530.9 2.7 fusion.119
  533.6 6.9 fusion.64
  540.5 6.9 fusion.19
  547.4 2.7 fusion.120
  550.1 6.6 fusion.65
  556.7 7.0 fusion.17
  564.8 1.6 multiply_add_fusion.1
  566.5 1.3 maximum_maximum_fusion
  567.8 5.1 convolution_multiply_fusion
  573.0 2.4 fusion.25
  575.4 1.5 fusion.72
  576.9 1.5 pad_maximum_fusion
  578.4 1.3 collective-permute-start
  579.7 3.9 select_select_fusion.7
  583.6 2.1 select_select_fusion.8
  585.7 40.9 %collective-permute-done = bf16[2,256,2048]{2,1,0:T(8,128)(2,1)} collective-permute-done((bf16[2,256,2048]{2,1,0:T(8,128)(2,1)}, bf16[2,256,2048]{2,1,0:T(8,128)(2,1)}, u32[]{:S(2)}, u32[]{:S(2)}) %collective-permute-start) | collective-permute-done | bytes 2097184 | tf_op jit(solution)/shard_map/while/body/eval_jaxpr/ppermute | solution.py:21
  626.9 4.4 convolution_convert_fusion.2
  631.3 3.9 bitcast_convert_fusion
  635.2 12.7 %pad_maximum_fusion.1 = bf16[2048,2560]{0,1:T(8,128)(2,1)} fusion(bf16[2048,1024]{0,1:T(8,128)(2,1)S(1)} %convolution_convert_fusion.2, bf16[2048,1536]{0,1:T(8,128)(2,1)S(1)} %bitcast_convert_fusion), kind=kLoop, calls=%fused_computation.119 | loop fusion | flops 20971520 | bytes 20971520 | tf_op jit(solution)/shard_map/concatenate | solution.py:216
  647.9 106.5 %reduce-scatter.2.cloned.1.call-done = bf16[256,2560]{0,1:T(8,128)(2,1)} async-done(((bf16[2048,2560]{0,1:T(8,128)(2,1)}), bf16[256,2560]{0,1:T(8,128)(2,1)}) %reduce-scatter.2.cloned.1.call-update) | async-done | bytes 1310736 | tf_op jit(solution)/shard_map/reduce_scatter | solution.py:215
  754.5 1.3 slice_bitcast_fusion
  (151 shorter events, 18.5 us)
Async XLA Ops:
  7.2 6.5 copy-start.22
  7.2 27.3 %all-gather.9.cloned.1.call-start = ((), (), s32[]{:S(2)}) async-start(), calls=%async_computation.3 | async-start | bytes 1179648 | tf_op jit(solution)/shard_map/all_gather | solution.py:158
  7.9 49.9 %all-gather.11.cloned.1.call-start = ((), (), s32[]{:S(2)}) async-start(), calls=%async_computation.4 | async-start | bytes 1179648 | tf_op jit(solution)/shard_map/all_gather | solution.py:159
  8.7 97.5 %all-gather.7.cloned.1.call-start = ((), (), s32[]{:S(2)}) async-start(), calls=%async_computation.2 | async-start | bytes 4718592 | tf_op jit(solution)/shard_map/all_gather | solution.py:157
  9.4 144.2 %all-gather.5.cloned.1.call-start = ((), (), s32[]{:S(2)}) async-start(), calls=%async_computation.1 | async-start | bytes 4718592 | tf_op jit(solution)/shard_map/all_gather | solution.py:160
  10.0 744.5 %reduce-scatter.2.cloned.1.call-start = ((), (), s32[]{:S(2)}) async-start(), calls=%async_computation.5 | async-start | bytes 11796480 | tf_op jit(solution)/shard_map/reduce_scatter | solution.py:215
  12.5 6.7 copy-start.16
  23.7 1.9 copy-start.11
  25.6 2.4 copy-start
  155.2 3.8 copy-start.6
  155.2 3.8 copy-start.13
  155.3 3.7 copy-start.17
  155.3 3.7 copy-start.25
  161.9 50.0 %collective-permute-start = (bf16[2,256,2048]{2,1,0:T(8,128)(2,1)}, bf16[2,256,2048]{2,1,0:T(8,128)(2,1)}, u32[]{:S(2)}, u32[]{:S(2)}) collective-permute-start(bf16[2,256,2048]{2,1,0:T(8,128)(2,1)} %get-tuple-element.918), channel_id=1, source_target_pairs={{8,0},{16,8},{24,16},{9,1},{17,9},{25,17},{10,2},{18,10},{26,18},{... | collective-permute-start | bytes 6291464 | tf_op jit(solution)/shard_map/while/body/eval_jaxpr/ppermute | solution.py:21
  163.2 1.9 copy-start.3
  165.1 46.8 %copy-start.7 = (bf16[2,256,1024]{1,2,0:T(8,128)(2,1)S(1)}, bf16[2,256,1024]{1,2,0:T(8,128)(2,1)}, u32[]{:S(2)}) copy-start(bf16[2,256,1024]{1,2,0:T(8,128)(2,1)} %copy-done.6) | copy-start | bytes 3145732 | tf_op jit(solution)/shard_map/while
  165.1 46.8 %copy-start.14 = (bf16[2,256,256]{1,2,0:T(8,128)(2,1)S(1)}, bf16[2,256,256]{1,2,0:T(8,128)(2,1)}, u32[]{:S(2)}) copy-start(bf16[2,256,256]{1,2,0:T(8,128)(2,1)} %copy-done.13) | copy-start | bytes 786436 | tf_op jit(solution)/shard_map/while
  165.7 46.1 %copy-start.4 = (bf16[2,256,1536]{1,2,0:T(8,128)(2,1)}, bf16[2,256,1536]{1,2,0:T(8,128)(2,1)S(1)}, u32[]{:S(2)}) copy-start(bf16[2,256,1536]{1,2,0:T(8,128)(2,1)S(1)} %select_select_fusion.8) | copy-start | bytes 4718596 | tf_op jit(solution)/shard_map/while
  211.9 4.4 copy-start.6
  211.9 4.4 copy-start.13
  212.0 4.3 copy-start.17
  212.0 4.3 copy-start.25
  219.2 49.8 %collective-permute-start = (bf16[2,256,2048]{2,1,0:T(8,128)(2,1)}, bf16[2,256,2048]{2,1,0:T(8,128)(2,1)}, u32[]{:S(2)}, u32[]{:S(2)}) collective-permute-start(bf16[2,256,2048]{2,1,0:T(8,128)(2,1)} %get-tuple-element.918), channel_id=1, source_target_pairs={{8,0},{16,8},{24,16},{9,1},{17,9},{25,17},{10,2},{18,10},{26,18},{... | collective-permute-start | bytes 6291464 | tf_op jit(solution)/shard_map/while/body/eval_jaxpr/ppermute | solution.py:21
  220.5 3.3 copy-start.3
  223.7 45.2 %copy-start.7 = (bf16[2,256,1024]{1,2,0:T(8,128)(2,1)S(1)}, bf16[2,256,1024]{1,2,0:T(8,128)(2,1)}, u32[]{:S(2)}) copy-start(bf16[2,256,1024]{1,2,0:T(8,128)(2,1)} %copy-done.6) | copy-start | bytes 3145732 | tf_op jit(solution)/shard_map/while
  223.7 45.2 %copy-start.14 = (bf16[2,256,256]{1,2,0:T(8,128)(2,1)S(1)}, bf16[2,256,256]{1,2,0:T(8,128)(2,1)}, u32[]{:S(2)}) copy-start(bf16[2,256,256]{1,2,0:T(8,128)(2,1)} %copy-done.13) | copy-start | bytes 786436 | tf_op jit(solution)/shard_map/while
  224.4 44.6 %copy-start.4 = (bf16[2,256,1536]{1,2,0:T(8,128)(2,1)}, bf16[2,256,1536]{1,2,0:T(8,128)(2,1)S(1)}, u32[]{:S(2)}) copy-start(bf16[2,256,1536]{1,2,0:T(8,128)(2,1)S(1)} %select_select_fusion.8) | copy-start | bytes 4718596 | tf_op jit(solution)/shard_map/while
  269.0 4.4 copy-start.6
  269.0 4.4 copy-start.13
  269.1 4.3 copy-start.17
  269.1 4.3 copy-start.25
  276.3 232.8 %collective-permute-start = (bf16[2,256,2048]{2,1,0:T(8,128)(2,1)}, bf16[2,256,2048]{2,1,0:T(8,128)(2,1)}, u32[]{:S(2)}, u32[]{:S(2)}) collective-permute-start(bf16[2,256,2048]{2,1,0:T(8,128)(2,1)} %get-tuple-element.918), channel_id=1, source_target_pairs={{8,0},{16,8},{24,16},{9,1},{17,9},{25,17},{10,2},{18,10},{26,18},{... | collective-permute-start | bytes 6291464 | tf_op jit(solution)/shard_map/while/body/eval_jaxpr/ppermute | solution.py:21
  277.6 3.3 copy-start.3
  280.9 228.3 %copy-start.7 = (bf16[2,256,1024]{1,2,0:T(8,128)(2,1)S(1)}, bf16[2,256,1024]{1,2,0:T(8,128)(2,1)}, u32[]{:S(2)}) copy-start(bf16[2,256,1024]{1,2,0:T(8,128)(2,1)} %copy-done.6) | copy-start | bytes 3145732 | tf_op jit(solution)/shard_map/while
  280.9 228.3 %copy-start.14 = (bf16[2,256,256]{1,2,0:T(8,128)(2,1)S(1)}, bf16[2,256,256]{1,2,0:T(8,128)(2,1)}, u32[]{:S(2)}) copy-start(bf16[2,256,256]{1,2,0:T(8,128)(2,1)} %copy-done.13) | copy-start | bytes 786436 | tf_op jit(solution)/shard_map/while
  281.5 227.6 %copy-start.4 = (bf16[2,256,1536]{1,2,0:T(8,128)(2,1)}, bf16[2,256,1536]{1,2,0:T(8,128)(2,1)S(1)}, u32[]{:S(2)}) copy-start(bf16[2,256,1536]{1,2,0:T(8,128)(2,1)S(1)} %select_select_fusion.8) | copy-start | bytes 4718596 | tf_op jit(solution)/shard_map/while
  509.2 4.4 copy-start.6
  509.2 4.4 copy-start.13
  509.3 4.3 copy-start.17
  509.3 4.3 copy-start.25
  513.6 0.7 copy-start.15
  513.7 5.6 copy-start.1
  513.7 5.5 copy-start.8
  526.8 3.1 copy-start.9
  533.6 6.9 copy-start.21
  547.4 2.7 copy-start.12
  556.7 7.0 copy-start.18
  556.7 8.1 %copy-start.10 = (f32[4,4,256,64]{2,3,1,0:T(8,128)S(1)}, f32[4,4,256,64]{2,3,1,0:T(8,128)}, u32[]{:S(2)}) copy-start(f32[4,4,256,64]{2,3,1,0:T(8,128)} %fusion.19) | copy-start | bytes 3145732 | tf_op jit(solution)/shard_map/while/body/eval_jaxpr/cond
  564.7 1.7 copy-start.19
  564.7 1.7 copy-start.20
  566.4 6.5 slice-start
  567.8 5.1 slice-start.1
  572.9 2.4 copy-start.2
  578.4 48.3 %collective-permute-start = (bf16[2,256,2048]{2,1,0:T(8,128)(2,1)}, bf16[2,256,2048]{2,1,0:T(8,128)(2,1)}, u32[]{:S(2)}, u32[]{:S(2)}) collective-permute-start(bf16[2,256,2048]{2,1,0:T(8,128)(2,1)} %get-tuple-element.918), channel_id=1, source_target_pairs={{8,0},{16,8},{24,16},{9,1},{17,9},{25,17},{10,2},{18,10},{26,18},{... | collective-permute-start | bytes 6291464 | tf_op jit(solution)/shard_map/while/body/eval_jaxpr/ppermute | solution.py:21
  579.7 3.9 copy-start.3
  583.6 43.1 %copy-start.7 = (bf16[2,256,1024]{1,2,0:T(8,128)(2,1)S(1)}, bf16[2,256,1024]{1,2,0:T(8,128)(2,1)}, u32[]{:S(2)}) copy-start(bf16[2,256,1024]{1,2,0:T(8,128)(2,1)} %copy-done.6) | copy-start | bytes 3145732 | tf_op jit(solution)/shard_map/while
  583.6 43.1 %copy-start.14 = (bf16[2,256,256]{1,2,0:T(8,128)(2,1)S(1)}, bf16[2,256,256]{1,2,0:T(8,128)(2,1)}, u32[]{:S(2)}) copy-start(bf16[2,256,256]{1,2,0:T(8,128)(2,1)} %copy-done.13) | copy-start | bytes 786436 | tf_op jit(solution)/shard_map/while
  585.7 40.9 %copy-start.4 = (bf16[2,256,1536]{1,2,0:T(8,128)(2,1)}, bf16[2,256,1536]{1,2,0:T(8,128)(2,1)S(1)}, u32[]{:S(2)}) copy-start(bf16[2,256,1536]{1,2,0:T(8,128)(2,1)S(1)} %select_select_fusion.8) | copy-start | bytes 4718596 | tf_op jit(solution)/shard_map/while
  626.9 4.4 copy-start.5
  626.9 4.4 copy-start.23
  626.9 4.4 copy-start.24
Sparse Core Ops, SparseCore 0:
  9.6 24.7 all-gather.8
  36.0 21.7 all-gather.10
  59.4 46.7 all-gather.6
  107.7 45.8 all-gather.4
  648.1 106.3 reduce-scatter.1
where the time goes:
time: 767 us
  waiting for transfers between devices  585 us (76%)
  other arithmetic  68 us (9%)
  matrix products  64.6 us (8%)
  local copies, waits for them, and re-layouts  29.2 us (4%)
  between operations  14 us (2%)
    ppermute x4, waiting for transfers between devices, passed_along(): return lax.ppermute(block, axis, route)  359 us
    reduce_scatter x1, waiting for transfers between devices, on_device(): lax.psum_scatter(jnp.concatenate([lax.dot_general(normed_flat, qkv_flat,...  107 us
    all_gather x1, waiting for transfers between devices, on_device(): lax.all_gather(query_weight, 'fsdp', axis=1, tiled=True)  48.4 us
    all_gather x1, waiting for transfers between devices, on_device(): lax.all_gather(output_weight, 'fsdp', axis=1, tiled=True)  39.4 us
    all_gather x1, waiting for transfers between devices, on_device(): lax.all_gather(value_weight, 'fsdp', axis=1, tiled=True)  23.3 us
    select_n x4, other arithmetic, turn(): upstream_store = jnp.where(active, upstream_all, upstream_store)  16.7 us
  transfers between devices with their start and end apart: 9, of which 9 were waited for; matrix products, arithmetic and copies ran while one was open for 5% of the time, Pallas kernels for 0%

commit v1 on v0

v1 whole, which is shorter than its diff:
```python
import math

import jax
import jax.numpy as jnp
from jax import lax
from jax.experimental import pallas as pl
from jax.experimental.pallas import tpu as pltpu
from jax.sharding import PartitionSpec as P

HEADS = 16
KVH = 4
HD = 64


norm_eps = 1e-05
rotary_base = 500000.0
masked_score = -1e30


def rotary_tables(length, head_size):
    half_size = head_size // 2
    inverse = jnp.exp(
        -(2.0 * jnp.arange(half_size, dtype=jnp.float32) / head_size) * math.log(rotary_base)
    )
    angles = jnp.arange(length, dtype=jnp.float32)[:, None] * inverse[None, :]
    return (jnp.cos(angles), jnp.sin(angles))


def norm_parts(inputs):
    inputs_f = inputs.astype(jnp.float32)
    scale_inv = lax.rsqrt(jnp.mean(inputs_f * inputs_f, axis=-1, keepdims=True) + norm_eps)
    return (inputs_f * scale_inv, scale_inv)


def forward_parts(inputs, queries, keys, values, gain_row):
    length = inputs.shape[0]
    groups = HEADS // KVH
    unit_rows, scale_inv = norm_parts(inputs)
    normed = (unit_rows * gain_row.astype(jnp.float32)).astype(jnp.bfloat16)
    query_grid = queries.reshape(length, KVH, groups, HD)
    key_grid = keys.reshape(length, KVH, HD)
    value_grid = values.reshape(length, KVH, HD)
    scores = jnp.einsum(
        "tkgd,skd->kgts", query_grid, key_grid, preferred_element_type=jnp.float32
    ) * (1.0 / math.sqrt(HD))
    causal = jnp.arange(length)[:, None] >= jnp.arange(length)[None, :]
    scores = jnp.where(causal, scores, masked_score)
    row_peak = jnp.max(scores, axis=-1, keepdims=True)
    weights = jnp.exp(scores - row_peak)
    attn_probs = (weights / jnp.sum(weights, axis=-1, keepdims=True)).astype(jnp.bfloat16)
    attn_out = jnp.einsum(
        "kgts,skd->tkgd", attn_probs, value_grid, preferred_element_type=jnp.float32
    )
    return (attn_probs, normed, attn_out.astype(jnp.bfloat16).reshape(length, -1))


def chain_kernel(
    cotangent_ref,
    out_full_ref,
    in_full_ref,
    probs_ref,
    keys_ref,
    values_ref,
    queries_ref,
    inputs_ref,
    scale_ref,
    gain_ref,
    table_ref,
    grad_ref,
    qkv_ref,
    upstream_ref,
    held,
    d_attn,
    scaled_rows,
    key_sums,
    value_sums,
    send_sem,
    recv_sem,
    local_sem,
):
    section = lax.axis_index("section")
    sections = lax.axis_size("section")
    is_last = section == sections - 1
    below = lax.rem(section + sections - 1, sections)
    above = lax.rem(section + 1, sections)
    micro_count, length, width = grad_ref.shape
    half_rows = length // 2
    shards = in_full_ref.shape[0]
    shard = in_full_ref.shape[2]
    groups = HEADS // KVH
    qd = HEADS * HD
    kvd = KVH * HD

    barrier = pltpu.get_barrier_semaphore()

    @pl.when(section < sections - 1)
    def _():
        pl.semaphore_signal(
            barrier, inc=1, device_id={"section": above}, device_id_type=pl.DeviceIdType.MESH
        )

    @pl.when(is_last)
    def _():
        own = pltpu.make_async_copy(cotangent_ref, held, local_sem)
        own.start()
        own.wait()

    @pl.when(section > 0)
    def _():
        pl.semaphore_wait(barrier, 1)

    def hop(micro, half):
        rows = pl.ds(half * half_rows, half_rows)
        return pltpu.make_async_remote_copy(
            src_ref=grad_ref.at[micro, rows],
            dst_ref=held.at[micro, rows],
            send_sem=send_sem.at[micro, half],
            recv_sem=recv_sem.at[micro, half],
            device_id={"section": below},
            device_id_type=pl.DeviceIdType.MESH,
        )

    front = lax.broadcasted_iota(jnp.int32, (half_rows, 2 * HD), 1) < HD
    front_ones = jnp.where(front, 1.0, 0.0).astype(jnp.bfloat16)
    back_ones = jnp.where(front, 0.0, 1.0).astype(jnp.bfloat16)

    def both_halves(block):
        return block + pltpu.roll(block, HD, 1)

    def one_micro(micro, carry):
        for half in (1, 0):
            rows = pl.ds(half * half_rows, half_rows)
            span = (half + 1) * half_rows

            @pl.when(section < sections - 1)
            def _():
                hop(micro, half).wait_recv()

            def attn_tile(tile, carry):
                columns = pl.ds(pl.multiple_of(tile * 256, 256), 256)
                d_attn[:, columns] = jnp.dot(
                    held[micro, rows, :],
                    out_full_ref[:, columns],
                    preferred_element_type=jnp.float32,
                ).astype(jnp.bfloat16)
                return carry

            lax.fori_loop(0, qd // 256, attn_tile, 0)
            table = table_ref[rows, :]
            kept = []
            for head in range(KVH):
                pairs = [
                    d_attn[:, (head * groups + 2 * i) * HD : (head * groups + 2 * i + 2) * HD]
                    for i in range(groups // 2)
                ]
                d_rows = jnp.concatenate(
                    [pair * ones for pair in pairs for ones in (front_ones, back_ones)], axis=0
                )
                probs = probs_ref[micro, head, :, rows, :span].reshape(groups * half_rows, span)
                d_probs = jnp.dot(
                    d_rows, values_ref[micro, head, :, :span], preferred_element_type=jnp.float32
                )
                probs_f = probs.astype(jnp.float32)
                row_inner = jnp.sum(probs_f * d_probs, axis=-1, keepdims=True)
                d_scores = (probs_f * (d_probs - row_inner)).astype(jnp.bfloat16)
                d_query = jnp.dot(
                    d_scores, keys_ref[micro, head, :span, :], preferred_element_type=jnp.float32
                )
                turned = [
                    both_halves(d_query[g * half_rows : (g + 1) * half_rows] * table)
                    for g in range(groups)
                ]
                for i in range(groups // 2):
                    start = (head * groups + 2 * i) * HD
                    qkv_ref[micro, rows, start : start + 2 * HD] = jnp.where(
                        front, turned[2 * i], turned[2 * i + 1]
                    ).astype(jnp.bfloat16)
                query_rows = queries_ref[micro, head, :, rows, :].reshape(
                    groups * half_rows, 2 * HD
                )
                across = (((0,), (0,)), ((), ()))
                d_key = lax.dot_general(
                    d_scores, query_rows, across, preferred_element_type=jnp.float32
                )
                d_value = lax.dot_general(
                    probs, d_rows, across, preferred_element_type=jnp.float32
                )
                if half == 1:
                    key_sums[head] = d_key[:half_rows]
                    value_sums[head] = d_value[:half_rows]
                    d_key = d_key[half_rows:]
                    d_value = d_value[half_rows:]
                else:
                    d_key = d_key + key_sums[head]
                    d_value = d_value + value_sums[head]
                kept.append((both_halves(d_key * table), both_halves(d_value)))
                if head % 2 == 1:
                    start = qd + (head - 1) * HD
                    for which in range(2):
                        at = start + which * kvd
                        qkv_ref[micro, rows, at : at + 2 * HD] = jnp.where(
                            front, kept[head - 1][which], kept[head][which]
                        ).astype(jnp.bfloat16)

            scale = scale_ref[micro, rows, :]

            def normed_tile(tile, inner):
                columns = pl.ds(pl.multiple_of(tile * shard, shard), shard)
                d_normed = jnp.dot(
                    qkv_ref[micro, rows, :], in_full_ref[tile], preferred_element_type=jnp.float32
                )
                scaled = d_normed * gain_ref[:, columns].astype(jnp.float32)
                scaled_rows[:, columns] = scaled
                unit = inputs_ref[micro, rows, columns].astype(jnp.float32) * scale
                return inner + jnp.sum(scaled * unit, axis=-1, keepdims=True)

            inner = lax.fori_loop(
                0, shards, normed_tile, jnp.zeros((half_rows, 1), jnp.float32)
            ) * (1.0 / width)

            def grad_tile(tile, carry):
                columns = pl.ds(pl.multiple_of(tile * shard, shard), shard)
                unit = inputs_ref[micro, rows, columns].astype(jnp.float32) * scale
                d_inputs = scale * (scaled_rows[:, columns] - unit * inner)
                grad_ref[micro, rows, columns] = (
                    held[micro, rows, columns].astype(jnp.float32) + d_inputs
                ).astype(jnp.bfloat16)
                return carry

            lax.fori_loop(0, shards, grad_tile, 0)

            @pl.when(section > 0)
            def _():
                hop(micro, half).start()

        return carry

    lax.fori_loop(0, micro_count, one_micro, 0)
    keep = pltpu.make_async_copy(held, upstream_ref, local_sem)
    keep.start()
    keep.wait()

    @pl.when(section > 0)
    def _():
        for micro in range(micro_count):
            for half in (1, 0):
                hop(micro, half).wait_send()


def chain(cotangent, out_full, in_full, probs, keys, values, queries, inputs, scale, gain, table):
    micro_count, length, width = inputs.shape
    half_rows = length // 2
    qd = HEADS * HD
    qkv_width = in_full.shape[1]
    vmem = pl.BlockSpec(memory_space=pltpu.VMEM)
    hbm = pl.BlockSpec(memory_space=pl.ANY)
    return pl.pallas_call(
        chain_kernel,
        out_shape=(
            jax.ShapeDtypeStruct((micro_count, length, width), jnp.bfloat16),
            jax.ShapeDtypeStruct((micro_count, length, qkv_width), jnp.bfloat16),
            jax.ShapeDtypeStruct((micro_count, length, width), jnp.bfloat16),
        ),
        in_specs=[hbm] + [vmem] * 10,
        out_specs=(vmem, vmem, hbm),
        scratch_shapes=[
            pltpu.VMEM((micro_count, length, width), jnp.bfloat16),
            pltpu.VMEM((half_rows, qd), jnp.bfloat16),
            pltpu.VMEM((half_rows, width), jnp.float32),
            pltpu.VMEM((KVH, half_rows, 2 * HD), jnp.float32),
            pltpu.VMEM((KVH, half_rows, 2 * HD), jnp.float32),
            pltpu.SemaphoreType.DMA((micro_count, 2)),
            pltpu.SemaphoreType.DMA((micro_count, 2)),
            pltpu.SemaphoreType.DMA,
        ],
        compiler_params=pltpu.CompilerParams(
            collective_id=0, has_side_effects=True, vmem_limit_bytes=52 * 2**20
        ),
        cost_estimate=pl.CostEstimate(
            flops=2 * micro_count * length * width * (qkv_width + qd),
            bytes_accessed=24 * 2**20,
            transcendentals=0,
        ),
    )(cotangent, out_full, in_full, probs, keys, values, queries, inputs, scale, gain, table)


def with_swapped(rows):
    half_size = HD // 2
    swapped = jnp.concatenate([rows[..., half_size:], rows[..., :half_size]], axis=-1)
    return jnp.concatenate([rows, swapped], axis=-1)


def on_device(
    saved_inputs,
    saved_queries,
    saved_keys,
    saved_values,
    cotangent,
    norm_gain,
    query_weight,
    key_weight,
    value_weight,
    output_weight,
):
    inputs = saved_inputs[0]
    queries = saved_queries[0]
    keys_all = saved_keys[0]
    values_all = saved_values[0]
    gain_row = norm_gain[0]
    micro_count = inputs.shape[0]
    length = inputs.shape[1]
    width = inputs.shape[2]
    groups = HEADS // KVH
    out_full = lax.all_gather(output_weight[0], "fsdp", axis=0, tiled=True)
    in_shard = jnp.concatenate([query_weight[0], key_weight[0], value_weight[0]], axis=1)
    in_full = lax.all_gather(in_shard.T, "fsdp", axis=0, tiled=False)
    qkv_width = in_shard.shape[1]
    forward_all = jax.vmap(forward_parts, in_axes=(0, 0, 0, 0, None))
    attn_probs, normed, attn_out = forward_all(inputs, queries, keys_all, values_all, gain_row)
    scale_inv = norm_parts(inputs)[1]
    cosine, sine = rotary_tables(length, HD)
    table = jnp.concatenate([cosine, cosine, sine, -sine], axis=1)
    query_grid = with_swapped(
        queries.reshape(micro_count, length, KVH, groups, HD).transpose(0, 2, 3, 1, 4)
    )
    key_grid = with_swapped(keys_all.reshape(micro_count, length, KVH, HD).transpose(0, 2, 1, 3))
    value_grid = values_all.reshape(micro_count, length, KVH, HD).transpose(0, 2, 3, 1)
    value_grid = value_grid * jnp.bfloat16(1.0 / math.sqrt(HD))
    value_grid = jnp.concatenate([value_grid, value_grid], axis=2)
    grads, qkv_all, upstream_all = chain(
        cotangent,
        out_full,
        in_full,
        attn_probs,
        key_grid,
        value_grid,
        query_grid,
        inputs,
        scale_inv,
        norm_gain,
        table,
    )
    normed_flat = normed.reshape(micro_count * length, width)
    qkv_flat = qkv_all.reshape(micro_count * length, qkv_width)
    attn_flat = attn_out.reshape(micro_count * length, -1)
    upstream_flat = upstream_all.reshape(micro_count * length, width)
    summed = lax.psum_scatter(
        jnp.concatenate(
            [
                lax.dot_general(
                    normed_flat,
                    qkv_flat,
                    (((0,), (0,)), ((), ())),
                    preferred_element_type=jnp.float32,
                ),
                lax.dot_general(
                    upstream_flat,
                    attn_flat,
                    (((0,), (0,)), ((), ())),
                    preferred_element_type=jnp.float32,
                ),
            ],
            axis=1,
        ).astype(jnp.bfloat16),
        "fsdp",
        scatter_dimension=0,
        tiled=True,
    )
    query_cols = query_weight.shape[2]
    key_cols = key_weight.shape[2]
    grad_query = summed[:, :query_cols]
    grad_key = summed[:, query_cols : query_cols + key_cols]
    grad_value = summed[:, query_cols + key_cols : qkv_width]
    grad_output = summed[:, qkv_width:]
    return (
        grads[None],
        grad_query[None],
        grad_key[None],
        grad_value[None],
        grad_output[None],
    )


def solution(mesh):
    return jax.shard_map(
        on_device,
        mesh=mesh,
        in_specs=(
            P("section", None, "fsdp", None),
            P("section", None, "fsdp", None),
            P("section", None, "fsdp", None),
            P("section", None, "fsdp", None),
            P(None, "fsdp", None),
            P("section", None),
            P("section", "fsdp", None),
            P("section", "fsdp", None),
            P("section", "fsdp", None),
            P("section", "fsdp", None),
        ),
        out_specs=(
            P("section", None, "fsdp", None),
            P("section", "fsdp", None),
            P("section", "fsdp", None),
            P("section", "fsdp", None),
            P("section", "fsdp", None),
        ),
        check_vma=False,
    )
```

time: 767 us -> 379 us (0.49)
  waiting for transfers between devices: 585 us -> 182 us
  Pallas kernels: 0 us -> 114 us
  matrix products: 64.6 us -> 16.8 us
  other arithmetic: 68 us -> 27.3 us
    ppermute x4 -> x0, waiting for transfers between devices: 359 us -> none  [passed_along(): return lax.ppermute(block, axis, route)]
    pallas_call x0 -> x1, Pallas kernels: none -> 114 us  [chain(): pl.pallas_call(chain_kernel, out_shape=(jax.ShapeDtypeStruct((micro_count...]
    dot_general x12 -> x0, matrix products: 50.5 us -> none  [the longest x2 13.9 us: backward_step(): jnp.einsum('kgts,skd->tkgd', d_scores, key_grid, preferred_element_type=j...]
    all_gather x4 -> x2, waiting for transfers between devices: 117 us -> 75.3 us  [the longest x1 38.8 us: on_device(): out_full = lax.all_gather(output_weight[0], 'fsdp', axis=0, tiled=True)]
    select_n x12 -> x0, other arithmetic: 32.6 us -> none  [the longest x4 16.7 us: turn(): upstream_store = jnp.where(active, upstream_all, upstream_store)]
    broadcast_in_dim x7 -> x0, local copies, waits for them, and re-layouts: 10.1 us -> none  [the longest x4 6.36 us: on_device(): grads_zero = jnp.zeros((micro_count, length, width), jnp.bfloat16)]
    all_gather x0 -> x1, local copies, waits for them, and re-layouts: none -> 8.69 us  [on_device(): in_full = lax.all_gather(in_shard.T, 'fsdp', axis=0, tiled=False)]
  transfers between devices with their start and end apart: 9 -> 3, of which waited for: 9 -> 3; matrix products, arithmetic and copies ran while one was open for 5% -> 10% of each run, Pallas kernels for 0% -> 0%
where the time goes in v1:
time: 379 us
  waiting for transfers between devices  182 us (48%)
  Pallas kernels  114 us (30%)
  other arithmetic  27.3 us (7%)
  local copies, waits for them, and re-layouts  24.7 us (7%)
  matrix products  16.8 us (4%)
  between operations  14 us (4%)
    pallas_call x1, Pallas kernels, chain(): pl.pallas_call(chain_kernel, out_shape=(jax.ShapeDtypeStruct((micro_count...  114 us
    reduce_scatter x1, waiting for transfers between devices, on_device(): lax.psum_scatter(jnp.concatenate([lax.dot_general(normed_flat, qkv_flat,...  106 us
    all_gather x1, waiting for transfers between devices, on_device(): out_full = lax.all_gather(output_weight[0], 'fsdp', axis=0, tiled=True)  38.8 us
    all_gather x1, waiting for transfers between devices, on_device(): in_full = lax.all_gather(in_shard.T, 'fsdp', axis=0, tiled=False)  36.5 us
    concatenate x1, other arithmetic, on_device(): jnp.concatenate([lax.dot_general(normed_flat, qkv_flat, (((0,), (0,)), ((...  12.4 us
    unnamed x27, local copies, waits for them, and re-layouts  9.97 us
    all_gather x1, local copies, waits for them, and re-layouts, on_device(): in_full = lax.all_gather(in_shard.T, 'fsdp', axis=0, tiled=False)  8.69 us
  transfers between devices with their start and end apart: 3, of which 3 were waited for; matrix products, arithmetic and copies ran while one was open for 10% of the time, Pallas kernels for 0%

profile of v1, /device:TPU:0, one launch (start us, length us, event | category | flops | bytes accessed | tf_op | source)
XLA Modules:
  0.0 378.8 jit_solution(5897256097055661311)
XLA Ops:
  7.2 0.0 all-gather.7.cloned.1.call-start
  7.2 2.1 maximum_bitcast_fusion
  9.3 0.0 all-gather.7.cloned.1.call-update
  9.4 0.0 all-gather.5.cloned.1.call-start
  9.4 0.7 all-gather.5.cloned.1.call-update
  10.1 0.0 reduce-scatter.2.cloned.1.call-start
  10.2 1.5 copy.41
  11.6 0.0 copy-start.4
  11.7 1.1 copy.45
  12.7 1.1 copy.40
  13.8 0.0 copy-done.4
  13.8 0.3 copy.43
  14.1 0.0 copy-start.3
  14.1 1.3 copy.44
  15.4 2.1 fusion.2
  17.5 0.6 add_rsqrt_fusion
  18.1 0.1 copy.47.scale_ref
  18.3 7.3 %fusion.23 = (f32[2,4,4,256]{3,2,1,0:T(4,128)S(1)}, f32[2,4,4,256,256]{4,3,2,1,0:T(8,128)}) fusion(pred[256,256]{1,0:T(8,128)(4,1)S(1)} %iota_compare_fusion, bf16[2,256,4,64,1]{1,3,4,2,0:T(8,128)(2,1)S(1)} %bitcast.84, bf16[2,256,4,4,64]{1,4,3,2,0:T(8,128)(2,1)} %bitcast.78), kind=kOutput, calls=%fused_computation.44 | convolution fusion | flops 276824320 | bytes 9797632 | tf_op jit(solution)/shard_map/vmap()/sub | solution.py:49
  25.5 4.4 %divide_convert_fusion.probs_ref = bf16[2,4,4,256,256]{4,3,2,1,0:T(8,128)(2,1)S(1)} fusion(f32[2,4,4,256,256]{4,3,2,1,0:T(8,128)} %get-tuple-element.40, f32[2,4,4,256]{3,2,1,0:T(4,128)S(1)} %get-tuple-element.39), kind=kLoop, calls=%fused_computation.4 | loop fusion | flops 4194304 | bytes 12615680 | tf_op jit(solution)/shard_map/vmap()/convert_element_type | solution.py:50
  29.9 0.0 copy-start.1
  29.9 0.0 copy-start
  29.9 1.4 fusion.11
  31.3 1.1 copy.49
  32.4 1.3 copy.58
  33.6 0.0 copy-done.1
  33.6 0.0 copy-done
  33.7 0.5 fusion.15
  34.2 0.2 pad_maximum_fusion.4.table_ref
  34.5 0.0 copy-done.3
  34.5 0.2 fusion.22
  34.7 1.6 pad_maximum_fusion.2.keys_ref
  36.3 0.9 fusion.21
  37.2 3.3 pad_maximum_fusion.1.queries_ref
  40.5 36.5 %all-gather.7.cloned.1.call-done = bf16[12288,256]{0,1:T(8,128)(2,1)} async-done(((bf16[1536,256]{0,1:T(8,128)(2,1)}), bf16[12288,256]{0,1:T(8,128)(2,1)}) %all-gather.7.cloned.1.call-update) | async-done | bytes 6291472 | tf_op jit(solution)/shard_map/all_gather | solution.py:316
  77.1 8.7 %copy.39 = bf16[12288,256]{1,0:T(8,128)(2,1)} copy(bf16[12288,256]{0,1:T(8,128)(2,1)} %all-gather.7.cloned.1.call-done) | data formatting | bytes 12582912 | tf_op jit(solution)/shard_map/all_gather | solution.py:316
  85.7 38.8 %all-gather.5.cloned.1.call-done = bf16[1,2048,1024]{2,1,0:T(8,128)(2,1)} async-done(((bf16[1,256,1024]{2,1,0:T(8,128)(2,1)}), bf16[1,2048,1024]{2,1,0:T(8,128)(2,1)}) %all-gather.5.cloned.1.call-update) | async-done | bytes 4194320 | tf_op jit(solution)/shard_map/all_gather | solution.py:314
  124.5 0.0 copy-start.6
  124.5 113.6 %shard_map.137 = (bf16[2,256,2048]{2,1,0:T(8,128)(2,1)}, bf16[2,256,1536]{2,1,0:T(8,128)(2,1)}, bf16[2,256,2048]{2,1,0:T(8,128)(2,1)}) custom-call(bf16[2,256,2048]{2,1,0:T(8,128)(2,1)} %cotangent_ref.1, bf16[2048,1024]{1,0:T(8,128)(2,1)} %bitcast.76, bf16[8,1536,256]{2,1,0:T(8,128)(2,1)} %bitcast.72, bf16[2,4,4,256,256]{4,3,2,1,0:T(8,128)(2,1)} %copy-done.1, ...), custom_call_target="tpu_custom_call" | custom-call | flops 5368709120 | bytes 25165824 | tf_op jit(solution)/shard_map/pallas_call | solution.py:257
  238.1 0.0 copy-done.6
  238.1 0.0 copy-start.2
  238.1 0.0 copy-start.7
  238.1 0.0 copy-start.8
  238.1 4.1 %convolution_convert_fusion = bf16[2048,1024]{0,1:T(8,128)(2,1)S(1)} fusion(bf16[512,1024]{0,1:T(8,128)(2,1)S(1)} %bitcast.85, bf16[512,2048]{1,0:T(8,128)(2,1)} %bitcast.90), kind=kOutput, calls=%fused_computation.15 | convolution fusion | flops 2149580800 | bytes 7340032 | tf_op jit(solution)/shard_map/dot_general | solution.py:356
  242.2 0.0 copy-done.2
  242.2 0.0 copy-done.7
  242.2 0.0 copy-done.8
  242.3 4.1 %bitcast_convert_fusion = bf16[2048,1536]{0,1:T(8,128)(2,1)S(1)} fusion(bf16[2,256,1536]{2,1,0:T(8,128)(2,1)S(1)} %copy-done.8, f32[2048]{0:T(1024)S(1)} %bitcast.89, f32[2,256]{1,0:T(2,128)S(1)} %copy-done.7, bf16[1,2,256,2048]{3,2,1,0:T(8,128)(2,1)S(1)} %copy-done.2), kind=kOutput, calls=%fused_computation.1 | convolution fusion | flops 3228565504 | bytes 9971712 | tf_op jit(solution)/shard_map/dot_general | solution.py:350
  246.3 12.4 %pad_maximum_fusion = bf16[2048,2560]{0,1:T(8,128)(2,1)} fusion(bf16[2048,1024]{0,1:T(8,128)(2,1)S(1)} %convolution_convert_fusion, bf16[2048,1536]{0,1:T(8,128)(2,1)S(1)} %bitcast_convert_fusion), kind=kLoop, calls=%fused_computation.2 | loop fusion | flops 20971520 | bytes 20971520 | tf_op jit(solution)/shard_map/concatenate | solution.py:348
  258.7 0.0 reduce-scatter.2.cloned.1.call-update
  258.8 0.0 copy-start.5
  258.8 106.4 %reduce-scatter.2.cloned.1.call-done = bf16[256,2560]{0,1:T(8,128)(2,1)} async-done(((bf16[2048,2560]{0,1:T(8,128)(2,1)}), bf16[256,2560]{0,1:T(8,128)(2,1)}) %reduce-scatter.2.cloned.1.call-update) | async-done | bytes 1310736 | tf_op jit(solution)/shard_map/reduce_scatter | solution.py:347
  365.2 1.3 slice_bitcast_fusion
  366.5 1.0 copy.50
  367.5 1.0 copy.53
  368.5 1.0 slice_bitcast_fusion.2
  369.5 0.8 copy.51
  370.2 0.8 copy.52
  371.0 0.0 copy-done.5
  371.0 1.3 copy.60
  (5 shorter events, 0.1 us)
Async XLA Ops:
  7.2 69.9 %all-gather.7.cloned.1.call-start = ((), (), s32[]{:S(2)}) async-start(), calls=%async_computation.3 | async-start | bytes 7077888 | tf_op jit(solution)/shard_map/all_gather | solution.py:316
  9.4 115.2 %all-gather.5.cloned.1.call-start = ((), (), s32[]{:S(2)}) async-start(), calls=%async_computation.2 | async-start | bytes 4718592 | tf_op jit(solution)/shard_map/all_gather | solution.py:314
  10.1 355.1 %reduce-scatter.2.cloned.1.call-start = ((), (), s32[]{:S(2)}) async-start(), calls=%async_computation.1 | async-start | bytes 11796480 | tf_op jit(solution)/shard_map/reduce_scatter | solution.py:347
  11.6 2.2 copy-start.4
  14.1 20.3 %copy-start.3 = (bf16[2,256,4,64]{3,1,2,0:T(8,128)(2,1)}, bf16[2,256,4,64]{3,1,2,0:T(8,128)(2,1)S(1)}, u32[]{:S(2)}) copy-start(bf16[2,256,4,64]{3,1,2,0:T(8,128)(2,1)S(1)} %copy.43) | copy-start | bytes 786436
  29.9 3.8 copy-start.1
  29.9 3.7 copy-start
  124.5 113.6 %copy-start.6 = (bf16[128,8,2,256]{3,1,2,0:T(8,128)(2,1)S(1)}, bf16[128,8,2,256]{3,1,2,0:T(8,128)(2,1)}, u32[]{:S(2)}) copy-start(bf16[128,8,2,256]{3,1,2,0:T(8,128)(2,1)} %copy.58) | copy-start | bytes 3145732
  238.1 4.1 %copy-start.2 = (bf16[1,2,256,2048]{3,2,1,0:T(8,128)(2,1)S(1)}, bf16[1,2,256,2048]{3,2,1,0:T(8,128)(2,1)}, u32[]{:S(2)}) copy-start(bf16[1,2,256,2048]{3,2,1,0:T(8,128)(2,1)} %param.10) | copy-start | bytes 6291460
  238.1 4.1 %copy-start.7 = (f32[2,256]{1,0:T(2,128)S(1)}, f32[2,256]{1,0:T(2,128)}, u32[]{:S(2)}) copy-start(f32[2,256]{1,0:T(2,128)} %get-tuple-element.34) | copy-start | bytes 6148
  238.1 4.1 %copy-start.8 = (bf16[2,256,1536]{2,1,0:T(8,128)(2,1)S(1)}, bf16[2,256,1536]{2,1,0:T(8,128)(2,1)}, u32[]{:S(2)}) copy-start(bf16[2,256,1536]{2,1,0:T(8,128)(2,1)} %get-tuple-element.9) | copy-start | bytes 4718596
  258.8 112.2 %copy-start.5 = (bf16[2,256,2048]{2,1,0:T(8,128)(2,1)S(1)}, bf16[2,256,2048]{2,1,0:T(8,128)(2,1)}, u32[]{:S(2)}) copy-start(bf16[2,256,2048]{2,1,0:T(8,128)(2,1)} %get-tuple-element.8) | copy-start | bytes 6291460
Sparse Core Ops, SparseCore 0:
  9.6 67.4 all-gather.6
  78.7 45.8 all-gather.4
  258.9 106.2 reduce-scatter.1

commit v2 on v1

--- a/solution.py
+++ b/solution.py
@@ -290,6 +290,272 @@
     return jnp.concatenate([rows, swapped], axis=-1)
 
 
+def reduce_kernel(
+    normed_ref,
+    qkv_ref,
+    upstream_ref,
+    attn_ref,
+    out_ref,
+    for_twin,
+    from_twin,
+    stage,
+    line,
+    other,
+    twin_send,
+    twin_recv,
+    line_send,
+    line_recv,
+    other_recv,
+):
+    mine = lax.axis_index("fsdp")
+    place = mine // 2
+    core = mine % 2
+    places, shard, columns_out = stage.shape
+    qkv_width = qkv_ref.shape[1]
+    twin = place * 2 + 1 - core
+    lower = lax.rem(place + places - 1, places) * 2 + core
+    upper = lax.rem(place + 1, places) * 2 + core
+    has_lower = place > 0
+    has_upper = place < places - 1
+    mesh_id = pl.DeviceIdType.MESH
+
+    barrier = pltpu.get_barrier_semaphore()
+    pl.semaphore_signal(barrier, inc=1, device_id={"fsdp": twin}, device_id_type=mesh_id)
+
+    @pl.when(has_lower)
+    def _():
+        pl.semaphore_signal(barrier, inc=1, device_id={"fsdp": lower}, device_id_type=mesh_id)
+
+    @pl.when(has_upper)
+    def _():
+        pl.semaphore_signal(barrier, inc=1, device_id={"fsdp": upper}, device_id_type=mesh_id)
+
+    @pl.when(jnp.logical_and(has_lower, has_upper))
+    def _():
+        pl.semaphore_wait(barrier, 3)
+
+    @pl.when(jnp.logical_not(jnp.logical_and(has_lower, has_upper)))
+    def _():
+        pl.semaphore_wait(barrier, 2)
+
+    def remote(source, target, send, recv, device):
+        return pltpu.make_async_remote_copy(
+            src_ref=source,
+            dst_ref=target,
+            send_sem=send,
+            recv_sem=recv,
+            device_id={"fsdp": device},
+            device_id_type=mesh_id,
+        )
+
+    def to_twin(t):
+        return remote(for_twin.at[t], from_twin.at[t], twin_send.at[t], twin_recv.at[t], twin)
+
+    def go_up(t):
+        return remote(stage.at[t], line.at[t], line_send.at[t], line_recv.at[t], upper)
+
+    def go_down(t):
+        return remote(stage.at[t], line.at[t], line_send.at[t], line_recv.at[t], lower)
+
+    def end_down(t):
+        return remote(stage.at[t], other, line_send.at[t], other_recv, lower)
+
+    across = (((0,), (0,)), ((), ()))
+
+    def partial(t, which_core, store):
+        rows = pl.ds(pl.multiple_of((t * 2 + which_core) * shard, shard), shard)
+
+        def qkv_tile(tile, carry):
+            columns = pl.ds(pl.multiple_of(tile * 512, 512), 512)
+            store(
+                columns,
+                lax.dot_general(
+                    normed_ref[:, rows],
+                    qkv_ref[:, columns],
+                    across,
+                    preferred_element_type=jnp.float32,
+                ),
+            )
+            return carry
+
+        def out_tile(tile, carry):
+            columns = pl.ds(pl.multiple_of(tile * 512, 512), 512)
+            store(
+                pl.ds(pl.multiple_of(qkv_width + tile * 512, 512), 512),
+                lax.dot_general(
+                    upstream_ref[:, rows],
+                    attn_ref[:, columns],
+                    across,
+                    preferred_element_type=jnp.float32,
+                ),
+            )
+            return carry
+
+        lax.fori_loop(0, qkv_width // 512, qkv_tile, 0)
+        lax.fori_loop(0, attn_ref.shape[1] // 512, out_tile, 0)
+
+    low_half = place < places // 2
+
+    def target(step):
+        return jnp.where(low_half, places - 1 - step, step)
+
+    def send_twin(step, carry):
+        t = target(step)
+
+        def store(columns, block):
+            for_twin[t, :, columns] = block.astype(jnp.bfloat16)
+
+        partial(t, 1 - core, store)
+        to_twin(t).start()
+        return carry
+
+    lax.fori_loop(0, places, send_twin, 0)
+
+    def chip_sum(step, carry):
+        t = target(step)
+        to_twin(t).wait_recv()
+
+        def store(columns, block):
+            stage[t, :, columns] = (
+                block + from_twin[t, :, columns].astype(jnp.float32)
+            ).astype(jnp.bfloat16)
+
+        partial(t, core, store)
+
+        @pl.when(jnp.logical_and(place == 0, t > place))
+        def _():
+            go_up(t).start()
+
+        @pl.when(jnp.logical_and(place == places - 1, t < place - 1))
+        def _():
+            go_down(t).start()
+
+        @pl.when(jnp.logical_and(place == places - 1, t == place - 1))
+        def _():
+            end_down(t).start()
+
+        return carry
+
+    lax.fori_loop(0, places, chip_sum, 0)
+
+    def add_line(t):
+        def tile(tile, carry):
+            columns = pl.ds(pl.multiple_of(tile * 512, 512), 512)
+            stage[t, :, columns] = (
+                stage[t, :, columns].astype(jnp.float32) + line[t, :, columns].astype(jnp.float32)
+            ).astype(jnp.bfloat16)
+            return carry
+
+        lax.fori_loop(0, columns_out // 512, tile, 0)
+
+    def relay(tick, carry):
+        @pl.when(jnp.logical_and(has_lower, place <= tick))
+        def _():
+            t = places - 1 - tick + place
+            go_up(t).wait_recv()
+            add_line(t)
+            go_up(t).start()
+
+        @pl.when(jnp.logical_and(has_upper, tick >= places - 1 - place))
+        def _():
+            t = tick - (places - 1 - place)
+            go_down(t).wait_recv()
+            add_line(t)
+
+            @pl.when(t < place - 1)
+            def _():
+                go_down(t).start()
+
+            @pl.when(t == place - 1)
+            def _():
+                end_down(t).start()
+
+        return carry
+
+    lax.fori_loop(0, places - 1, relay, 0)
+
+    @pl.when(has_lower)
+    def _():
+        go_up(place).wait_recv()
+
+    @pl.when(has_upper)
+    def _():
+        end_down(place).wait_recv()
+
+    def finish(tile, carry):
+        columns = pl.ds(pl.multiple_of(tile * 512, 512), 512)
+        total = stage[place, :, columns].astype(jnp.float32)
+
+        @pl.when(jnp.logical_not(has_lower))
+        def _():
+            out_ref[:, columns] = (total + other[:, columns].astype(jnp.float32)).astype(
+                jnp.bfloat16
+            )
+
+        @pl.when(jnp.logical_not(has_upper))
+        def _():
+            out_ref[:, columns] = (total + line[place, :, columns].astype(jnp.float32)).astype(
+                jnp.bfloat16
+            )
+
+        @pl.when(jnp.logical_and(has_lower, has_upper))
+        def _():
+            out_ref[:, columns] = (
+                total
+                + line[place, :, columns].astype(jnp.float32)
+                + other[:, columns].astype(jnp.float32)
+            ).astype(jnp.bfloat16)
+
+        return carry
+
+    lax.fori_loop(0, columns_out // 512, finish, 0)
+
+    def sent(t, carry):
+        to_twin(t).wait_send()
+
+        @pl.when(t != place)
+        def _():
+            go_up(t).wait_send()
+
+        return carry
+
+    lax.fori_loop(0, places, sent, 0)
+
+
+def weight_grads(normed, qkv, upstream, attn):
+    tokens, width = normed.shape
+    devices = lax.axis_size("fsdp")
+    places = devices // 2
+    shard = width // devices
+    columns = qkv.shape[1] + attn.shape[1]
+    vmem = pl.BlockSpec(memory_space=pltpu.VMEM)
+    block = pltpu.VMEM((places, shard, columns), jnp.bfloat16)
+    return pl.pallas_call(
+        reduce_kernel,
+        out_shape=jax.ShapeDtypeStruct((shard, columns), jnp.bfloat16),
+        in_specs=[vmem] * 4,
+        out_specs=vmem,
+        scratch_shapes=[
+            block,
+            block,
+            block,
+            block,
+            pltpu.VMEM((shard, columns), jnp.bfloat16),
+            pltpu.SemaphoreType.DMA((places,)),
+            pltpu.SemaphoreType.DMA((places,)),
+            pltpu.SemaphoreType.DMA((places,)),
+            pltpu.SemaphoreType.DMA((places,)),
+            pltpu.SemaphoreType.DMA,
+        ],
+        compiler_params=pltpu.CompilerParams(
+            collective_id=1, has_side_effects=True, vmem_limit_bytes=52 * 2**20
+        ),
+        cost_estimate=pl.CostEstimate(
+            flops=2 * tokens * width * columns, bytes_accessed=8 * 2**20, transcendentals=0
+        ),
+    )(normed, qkv, upstream, attn)
+
+
 def on_device(
     saved_inputs,
     saved_queries,
@@ -344,28 +610,7 @@
     qkv_flat = qkv_all.reshape(micro_count * length, qkv_width)
     attn_flat = attn_out.reshape(micro_count * length, -1)
     upstream_flat = upstream_all.reshape(micro_count * length, width)
-    summed = lax.psum_scatter(
-        jnp.concatenate(
-            [
-                lax.dot_general(
-                    normed_flat,
-                    qkv_flat,
-                    (((0,), (0,)), ((), ())),
-                    preferred_element_type=jnp.float32,
-                ),
-                lax.dot_general(
-                    upstream_flat,
-                    attn_flat,
-                    (((0,), (0,)), ((), ())),
-                    preferred_element_type=jnp.float32,
-                ),
-            ],
-            axis=1,
-        ).astype(jnp.bfloat16),
-        "fsdp",
-        scatter_dimension=0,
-        tiled=True,
-    )
+    summed = weight_grads(normed_flat, qkv_flat, upstream_flat, attn_flat)
     query_cols = query_weight.shape[2]
     key_cols = key_weight.shape[2]
     grad_query = summed[:, :query_cols]

time: 379 us -> 352 us (0.929)
  waiting for transfers between devices: 182 us -> 71.9 us
  Pallas kernels: 114 us -> 215 us
  other arithmetic: 27.3 us -> 14.3 us
  matrix products: 16.8 us -> 8.26 us
    reduce_scatter x1 -> x0, waiting for transfers between devices: 106 us -> none  [on_device(): lax.psum_scatter(jnp.concatenate([lax.dot_general(normed_flat, qkv_flat,...]
    pallas_call x0 -> x1, Pallas kernels: none -> 102 us  [weight_grads(): pl.pallas_call(reduce_kernel, out_shape=jax.ShapeDtypeStruct((shard, colu...]
    concatenate x1 -> x0, other arithmetic: 12.4 us -> none  [on_device(): jnp.concatenate([lax.dot_general(normed_flat, qkv_flat, (((0,), (0,)), ((...]
    dot_general x2 -> x0, matrix products: 8.13 us -> none  [the longest x1 4.08 us: on_device(): lax.dot_general(upstream_flat, attn_flat, (((0,), (0,)), ((), ())), prefe...]
    all_gather x1, waiting for transfers between devices: 36.5 us -> 32.4 us  [on_device(): in_full = lax.all_gather(in_shard.T, 'fsdp', axis=0, tiled=False)]
    unnamed x27 -> x25, local copies, waits for them, and re-layouts: 9.97 us -> 7.64 us
  transfers between devices with their start and end apart: 3 -> 2, of which waited for: 3 -> 2; matrix products, arithmetic and copies ran while one was open for 10% -> 11% of each run, Pallas kernels for 0% -> 0%
where the time goes in v2:
time: 352 us
  Pallas kernels  215 us (61%)
  waiting for transfers between devices  71.9 us (20%)
  local copies, waits for them, and re-layouts  28 us (8%)
  other arithmetic  14.3 us (4%)
  between operations  14.3 us (4%)
  matrix products  8.26 us (2%)
    pallas_call x1, Pallas kernels, chain(): pl.pallas_call(chain_kernel, out_shape=(jax.ShapeDtypeStruct((micro_count...  113 us
    pallas_call x1, Pallas kernels, weight_grads(): pl.pallas_call(reduce_kernel, out_shape=jax.ShapeDtypeStruct((shard, colu...  102 us
    all_gather x1, waiting for transfers between devices, on_device(): out_full = lax.all_gather(output_weight[0], 'fsdp', axis=0, tiled=True)  38.8 us
    all_gather x1, waiting for transfers between devices, on_device(): in_full = lax.all_gather(in_shard.T, 'fsdp', axis=0, tiled=False)  32.4 us
    all_gather x1, local copies, waits for them, and re-layouts, on_device(): in_full = lax.all_gather(in_shard.T, 'fsdp', axis=0, tiled=False)  8.68 us
    unnamed x25, local copies, waits for them, and re-layouts  7.64 us
  transfers between devices with their start and end apart: 2, of which 2 were waited for; matrix products, arithmetic and copies ran while one was open for 11% of the time, Pallas kernels for 0%

profile of v2, /device:TPU:0, one launch (start us, length us, event | category | flops | bytes accessed | tf_op | source)
XLA Modules:
  0.0 352.0 jit_solution(8404675858329713202)
XLA Ops:
  7.2 0.0 copy-start.9
  7.2 0.0 all-gather.7.cloned.1.call-start
  7.2 2.2 maximum_bitcast_fusion
  9.4 0.0 all-gather.7.cloned.1.call-update
  9.4 0.0 all-gather.5.cloned.1.call-start
  9.5 0.7 all-gather.5.cloned.1.call-update
  10.2 0.0 copy-done.9
  10.2 0.5 copy.33
  10.7 0.0 copy-start.3
  10.8 1.8 copy.37
  12.5 1.1 copy.32
  13.6 0.0 copy-start.8
  13.6 1.0 copy.35
  14.6 1.8 copy.36
  16.4 0.0 copy-done.3
  16.4 0.5 multiply_reduce_fusion
  16.9 0.0 copy-done.8
  16.9 0.1 copy.39.scale_ref
  17.1 6.9 %fusion.19 = (f32[2,4,4,256]{3,2,1,0:T(4,128)S(1)}, f32[2,4,4,256,256]{4,3,2,1,0:T(8,128)}) fusion(pred[256,256]{1,0:T(8,128)(4,1)S(1)} %iota_compare_fusion, bf16[2,256,4,64,1]{1,3,4,2,0:T(8,128)(2,1)} %bitcast.76, bf16[2,256,4,4,64]{1,4,3,2,0:T(8,128)(2,1)S(1)} %bitcast.71), kind=kOutput, calls=%fused_computation.38 | convolution fusion | flops 276824320 | bytes 9797632 | tf_op jit(solution)/shard_map/vmap()/sub | solution.py:49
  24.0 0.0 copy-start.6
  24.0 4.2 %divide_convert_fusion.probs_ref = bf16[2,4,4,256,256]{4,3,2,1,0:T(8,128)(2,1)S(1)} fusion(f32[2,4,4,256,256]{4,3,2,1,0:T(8,128)} %get-tuple-element.25, f32[2,4,4,256]{3,2,1,0:T(4,128)S(1)} %get-tuple-element.24), kind=kLoop, calls=%fused_computation.2 | loop fusion | flops 4194304 | bytes 12615680 | tf_op jit(solution)/shard_map/vmap()/convert_element_type | solution.py:50
  28.2 0.0 copy-start.1
  28.2 2.0 copy-done.1
  30.2 0.0 copy-done.6
  30.2 1.4 fusion.7
  31.6 2.0 copy.45
  33.6 0.0 copy-start
  33.6 1.7 reshape.77.attn_ref
  35.2 0.0 copy-start.5
  35.3 0.0 copy-done
  35.3 0.5 fusion.11
  35.8 0.2 pad_maximum_fusion.3.table_ref
  36.0 1.0 multiply_bitcast_fusion
  37.0 0.0 copy-done.5
  37.0 0.0 copy-start.2
  37.0 0.2 fusion.18
  37.3 0.5 pad_maximum_fusion.1.keys_ref
  37.8 0.9 copy-done.2
  38.6 0.9 fusion.17
  39.5 0.0 copy-start.4
  39.5 3.3 pad_maximum_fusion.queries_ref
  42.8 0.0 copy-done.4
  42.8 1.9 fusion.3.normed_ref
  44.7 32.4 %all-gather.7.cloned.1.call-done = bf16[12288,256]{0,1:T(8,128)(2,1)} async-done(((bf16[1536,256]{0,1:T(8,128)(2,1)}), bf16[12288,256]{0,1:T(8,128)(2,1)}) %all-gather.7.cloned.1.call-update) | async-done | bytes 6291472 | tf_op jit(solution)/shard_map/all_gather | solution.py:582
  77.1 8.7 %copy.31 = bf16[12288,256]{1,0:T(8,128)(2,1)} copy(bf16[12288,256]{0,1:T(8,128)(2,1)} %all-gather.7.cloned.1.call-done) | data formatting | bytes 12582912 | tf_op jit(solution)/shard_map/all_gather | solution.py:582
  85.8 38.8 %all-gather.5.cloned.1.call-done = bf16[1,2048,1024]{2,1,0:T(8,128)(2,1)} async-done(((bf16[1,256,1024]{2,1,0:T(8,128)(2,1)}), bf16[1,2048,1024]{2,1,0:T(8,128)(2,1)}) %all-gather.5.cloned.1.call-update) | async-done | bytes 4194320 | tf_op jit(solution)/shard_map/all_gather | solution.py:580
  124.5 113.4 %shard_map.137 = (bf16[2,256,2048]{2,1,0:T(8,128)(2,1)}, bf16[2,256,1536]{2,1,0:T(8,128)(2,1)}, bf16[2,256,2048]{2,1,0:T(8,128)(2,1)}) custom-call(bf16[2,256,2048]{2,1,0:T(8,128)(2,1)} %cotangent_ref.1, bf16[2048,1024]{1,0:T(8,128)(2,1)} %bitcast.69, bf16[8,1536,256]{2,1,0:T(8,128)(2,1)} %bitcast.65, bf16[2,4,4,256,256]{4,3,2,1,0:T(8,128)(2,1)} %copy-done.1, ...), custom_call_target="tpu_custom_call" | custom-call | flops 5368709120 | bytes 25165824 | tf_op jit(solution)/shard_map/pallas_call | solution.py:257
  238.0 101.7 %shard_map.138 = bf16[256,2560]{1,0:T(8,128)(2,1)} custom-call(bf16[512,2048]{1,0:T(8,128)(2,1)} %fusion.3.normed_ref, bf16[512,1536]{1,0:T(8,128)(2,1)} %bitcast.83, bf16[512,2048]{1,0:T(8,128)(2,1)} %bitcast.82, bf16[512,1024]{1,0:T(8,128)(2,1)S(1)} %reshape.77.attn_ref), custom_call_target="tpu_custom_call" | custom-call | flops 5368709120 | bytes 8388608 | tf_op jit(solution)/shard_map/pallas_call | solution.py:533
  339.7 0.0 copy-start.7
  339.7 2.4 slice_bitcast_fusion
  342.1 1.7 slice_bitcast_fusion.2
  343.8 0.0 copy-done.7
  343.8 1.3 copy.49
  (6 shorter events, 0.1 us)
Async XLA Ops:
  7.2 3.0 copy-start.9
  7.2 69.9 %all-gather.7.cloned.1.call-start = ((), (), s32[]{:S(2)}) async-start(), calls=%async_computation.1 | async-start | bytes 7077888 | tf_op jit(solution)/shard_map/all_gather | solution.py:582
  9.4 115.1 %all-gather.5.cloned.1.call-start = ((), (), s32[]{:S(2)}) async-start(), calls=%async_computation | async-start | bytes 4718592 | tf_op jit(solution)/shard_map/all_gather | solution.py:580
  10.7 5.7 %copy-start.3 = (bf16[1,2,256,2048]{3,2,1,0:T(8,128)(2,1)S(1)}, bf16[1,2,256,2048]{3,2,1,0:T(8,128)(2,1)}, u32[]{:S(2)}) copy-start(bf16[1,2,256,2048]{3,2,1,0:T(8,128)(2,1)} %param.10) | copy-start | bytes 6291460
  13.6 3.3 copy-start.8
  24.0 6.2 %copy-start.6 = (bf16[1,2,256,256]{2,3,1,0:T(8,128)(2,1)S(1)}, bf16[1,2,256,256]{2,3,1,0:T(8,128)(2,1)}, u32[]{:S(2)}) copy-start(bf16[1,2,256,256]{2,3,1,0:T(8,128)(2,1)} %copy.36) | copy-start | bytes 786436
  28.2 2.0 copy-start.1
  33.6 1.7 copy-start
  35.2 1.8 copy-start.5
  37.0 1.6 copy-start.2
  39.5 3.3 copy-start.4
  339.7 4.1 %copy-start.7 = (bf16[2,256,2048]{2,1,0:T(8,128)(2,1)S(1)}, bf16[2,256,2048]{2,1,0:T(8,128)(2,1)}, u32[]{:S(2)}) copy-start(bf16[2,256,2048]{2,1,0:T(8,128)(2,1)} %get-tuple-element.8) | copy-start | bytes 6291460
Sparse Core Ops, SparseCore 0:
  9.6 67.4 all-gather.6
  78.7 45.8 all-gather.4

commit v3 on v2

--- a/solution.py
+++ b/solution.py
@@ -26,49 +26,28 @@
     return (jnp.cos(angles), jnp.sin(angles))
 
 
-def norm_parts(inputs):
-    inputs_f = inputs.astype(jnp.float32)
-    scale_inv = lax.rsqrt(jnp.mean(inputs_f * inputs_f, axis=-1, keepdims=True) + norm_eps)
-    return (inputs_f * scale_inv, scale_inv)
-
-
-def forward_parts(inputs, queries, keys, values, gain_row):
-    length = inputs.shape[0]
-    groups = HEADS // KVH
-    unit_rows, scale_inv = norm_parts(inputs)
-    normed = (unit_rows * gain_row.astype(jnp.float32)).astype(jnp.bfloat16)
-    query_grid = queries.reshape(length, KVH, groups, HD)
-    key_grid = keys.reshape(length, KVH, HD)
-    value_grid = values.reshape(length, KVH, HD)
-    scores = jnp.einsum(
-        "tkgd,skd->kgts", query_grid, key_grid, preferred_element_type=jnp.float32
-    ) * (1.0 / math.sqrt(HD))
-    causal = jnp.arange(length)[:, None] >= jnp.arange(length)[None, :]
-    scores = jnp.where(causal, scores, masked_score)
-    row_peak = jnp.max(scores, axis=-1, keepdims=True)
-    weights = jnp.exp(scores - row_peak)
-    attn_probs = (weights / jnp.sum(weights, axis=-1, keepdims=True)).astype(jnp.bfloat16)
-    attn_out = jnp.einsum(
-        "kgts,skd->tkgd", attn_probs, value_grid, preferred_element_type=jnp.float32
-    )
-    return (attn_probs, normed, attn_out.astype(jnp.bfloat16).reshape(length, -1))
-
-
 def chain_kernel(
     cotangent_ref,
+    out_shard_ref,
+    in_shard_ref,
+    saved_queries_ref,
+    saved_keys_ref,
+    saved_values_ref,
+    inputs_ref,
+    gain_ref,
+    table_ref,
+    grad_ref,
+    qkv_ref,
+    normed_ref,
+    attn_ref,
+    upstream_ref,
     out_full_ref,
     in_full_ref,
     probs_ref,
     keys_ref,
     values_ref,
     queries_ref,
-    inputs_ref,
     scale_ref,
-    gain_ref,
-    table_ref,
-    grad_ref,
-    qkv_ref,
-    upstream_ref,
     held,
     d_attn,
     scaled_rows,
@@ -77,6 +56,11 @@
     send_sem,
     recv_sem,
     local_sem,
+    up_send,
+    down_send,
+    twin_send,
+    line_recv,
+    twin_recv,
 ):
     section = lax.axis_index("section")
     sections = lax.axis_size("section")
@@ -90,14 +74,219 @@
     groups = HEADS // KVH
     qd = HEADS * HD
     kvd = KVH * HD
+    mesh_id = pl.DeviceIdType.MESH
+    mine = lax.axis_index("fsdp")
+    place = mine // 2
+    core = mine % 2
+    places = shards // 2
+    twin = place * 2 + 1 - core
+    lower = lax.rem(place + places - 1, places) * 2 + core
+    upper = lax.rem(place + 1, places) * 2 + core
+    has_lower = place > 0
+    has_upper = place < places - 1
 
     barrier = pltpu.get_barrier_semaphore()
+    pl.semaphore_signal(barrier, inc=1, device_id={"fsdp": twin}, device_id_type=mesh_id)
+
+    @pl.when(has_lower)
+    def _():
+        pl.semaphore_signal(barrier, inc=1, device_id={"fsdp": lower}, device_id_type=mesh_id)
+
+    @pl.when(has_upper)
+    def _():
+        pl.semaphore_signal(barrier, inc=1, device_id={"fsdp": upper}, device_id_type=mesh_id)
 
     @pl.when(section < sections - 1)
     def _():
-        pl.semaphore_signal(
-            barrier, inc=1, device_id={"section": above}, device_id_type=pl.DeviceIdType.MESH
+        pl.semaphore_signal(barrier, inc=1, device_id={"section": above}, device_id_type=mesh_id)
+
+    out_full_ref[mine] = out_shard_ref[...]
+    in_full_ref[mine] = in_shard_ref[...]
+    peers = (
+        1
+        + has_lower.astype(jnp.int32)
+        + has_upper.astype(jnp.int32)
+        + (section > 0).astype(jnp.int32)
+    )
+    pl.semaphore_wait(barrier, peers)
+
+    full_refs = (out_full_ref, in_full_ref)
+
+    def to_device(which, t, send, recv, device):
+        slot = t * 2 + core
+        return pltpu.make_async_remote_copy(
+            src_ref=full_refs[which].at[slot],
+            dst_ref=full_refs[which].at[slot],
+            send_sem=send.at[which, t],
+            recv_sem=recv.at[which, t],
+            device_id={"fsdp": device},
+            device_id_type=mesh_id,
         )
+
+    def go_up(which, t):
+        return to_device(which, t, up_send, line_recv, upper)
+
+    def go_down(which, t):
+        return to_device(which, t, down_send, line_recv, lower)
+
+    def to_twin(which, t):
+        return to_device(which, t, twin_send, twin_recv, twin)
+
+    def from_twin(which, t):
+        slot = t * 2 + 1 - core
+        return pltpu.make_async_remote_copy(
+            src_ref=full_refs[which].at[slot],
+            dst_ref=full_refs[which].at[slot],
+            send_sem=twin_send.at[which, t],
+            recv_sem=twin_recv.at[which, t],
+            device_id={"fsdp": twin},
+            device_id_type=mesh_id,
+        )
+
+    def gather_first(which):
+        @pl.when(has_upper)
+        def _():
+            go_up(which, place).start()
+
+        @pl.when(has_lower)
+        def _():
+            go_down(which, place).start()
+
+        to_twin(which, place).start()
+
+    def gather_step(which, step):
+        low = place - step
+        high = place + step
+
+        @pl.when(low >= 0)
+        def _():
+            go_up(which, low).wait_recv()
+
+            @pl.when(has_upper)
+            def _():
+                go_up(which, low).start()
+
+            to_twin(which, low).start()
+
+        @pl.when(high < places)
+        def _():
+            go_down(which, high).wait_recv()
+
+            @pl.when(has_lower)
+            def _():
+                go_down(which, high).start()
+
+            to_twin(which, high).start()
+
+    def gather_end(which):
+        def one(t, carry):
+            from_twin(which, t).wait_recv()
+            return carry
+
+        lax.fori_loop(0, places, one, 0)
+
+    def gather_sent(which):
+        def one(t, carry):
+            to_twin(which, t).wait_send()
+
+            @pl.when(jnp.logical_and(has_upper, t <= place))
+            def _():
+                go_up(which, t).wait_send()
+
+            @pl.when(jnp.logical_and(has_lower, t >= place))
+            def _():
+                go_down(which, t).wait_send()
+
+            return carry
+
+        lax.fori_loop(0, places, one, 0)
+
+    lanes = lax.broadcasted_iota(jnp.int32, (length, 2 * HD), 1)
+    front_all = lanes < HD
+    front_quarter = lax.rem(lanes, HD) < HD // 2
+    causal = lax.broadcasted_iota(jnp.int32, (length, length), 0) >= lax.broadcasted_iota(
+        jnp.int32, (length, length), 1
+    )
+    last_dims = (((1,), (1,)), ((), ()))
+
+    def swapped(block):
+        return jnp.where(
+            front_quarter,
+            pltpu.roll(block, 2 * HD - HD // 2, 1),
+            pltpu.roll(block, HD // 2, 1),
+        )
+
+    def one_head(own, beside, odd):
+        if odd:
+            return jnp.where(front_all, pltpu.roll(own, HD, 1), beside)
+        return jnp.where(front_all, own, pltpu.roll(beside, HD, 1))
+
+    def forward(micro):
+        def square_tile(tile, total):
+            columns = pl.ds(pl.multiple_of(tile * 256, 256), 256)
+            block = inputs_ref[micro, :, columns].astype(jnp.float32)
+            return total + jnp.sum(block * block, axis=-1, keepdims=True)
+
+        total = lax.fori_loop(
+            0, width // 256, square_tile, jnp.zeros((length, 1), jnp.float32)
+        )
+        scale_ref[micro] = lax.rsqrt(total * (1.0 / width) + norm_eps)
+
+        def unit_tile(tile, carry):
+            columns = pl.ds(pl.multiple_of(tile * 256, 256), 256)
+            unit = inputs_ref[micro, :, columns].astype(jnp.float32) * scale_ref[micro]
+            normed_ref[micro, :, columns] = (
+                unit * gain_ref[:, columns].astype(jnp.float32)
+            ).astype(jnp.bfloat16)
+            return carry
+
+        lax.fori_loop(0, width // 256, unit_tile, 0)
+
+        def head_pair(pair, carry):
+            columns = pl.ds(pl.multiple_of(pair * 2 * HD, 2 * HD), 2 * HD)
+            key_block = saved_keys_ref[micro, :, columns].astype(jnp.float32)
+            key_swapped = swapped(key_block)
+            value_block = saved_values_ref[micro, :, columns].astype(jnp.float32)
+            for odd in range(2):
+                head = pair * 2 + odd
+                key_rows = one_head(key_block, key_swapped, odd)
+                keys_ref[micro, head] = key_rows.astype(jnp.bfloat16)
+                key_alone = jnp.where(front_all, key_rows, 0.0).astype(jnp.bfloat16)
+                value_rows = one_head(value_block, value_block, odd).astype(jnp.bfloat16)
+                values_ref[micro, head] = value_rows
+                for i in range(groups // 2):
+                    start = pl.multiple_of((head * groups + 2 * i) * HD, 2 * HD)
+                    query_block = saved_queries_ref[micro, :, pl.ds(start, 2 * HD)].astype(
+                        jnp.float32
+                    )
+                    query_swapped = swapped(query_block)
+                    outs = []
+                    for second in range(2):
+                        query_rows = one_head(query_block, query_swapped, second).astype(
+                            jnp.bfloat16
+                        )
+                        queries_ref[micro, head, 2 * i + second] = query_rows
+                        scores = lax.dot_general(
+                            query_rows, key_alone, last_dims, preferred_element_type=jnp.float32
+                        ) * (1.0 / math.sqrt(HD))
+                        scores = jnp.where(causal, scores, masked_score)
+                        row_peak = jnp.max(scores, axis=-1, keepdims=True)
+                        weights = jnp.exp(scores - row_peak)
+                        probs = (weights / jnp.sum(weights, axis=-1, keepdims=True)).astype(
+                            jnp.bfloat16
+                        )
+                        probs_ref[micro, head, 2 * i + second] = probs
+                        outs.append(
+                            jnp.dot(probs, value_rows, preferred_element_type=jnp.float32)
+                        )
+                    attn_ref[micro, :, pl.ds(start, 2 * HD)] = jnp.where(
+                        front_all, outs[0], outs[1]
+                    ).astype(jnp.bfloat16)
+            return carry
+
+        lax.fori_loop(0, KVH // 2, head_pair, 0)
+
+    gather_first(0)
 
     @pl.when(is_last)
     def _():
@@ -105,9 +294,17 @@
         own.start()
         own.wait()
 
-    @pl.when(section > 0)
-    def _():
-        pl.semaphore_wait(barrier, 1)
+    for step in range(1, places):
+        if step <= micro_count:
+            forward(step - 1)
+        gather_step(0, step)
+    for micro in range(max(places - 1, 0), micro_count):
+        forward(micro)
+    gather_first(1)
+    gather_end(0)
+    for step in range(1, places):
+        gather_step(1, step)
+    gather_end(1)
 
     def hop(micro, half):
         rows = pl.ds(half * half_rows, half_rows)
@@ -140,7 +337,7 @@
                 columns = pl.ds(pl.multiple_of(tile * 256, 256), 256)
                 d_attn[:, columns] = jnp.dot(
                     held[micro, rows, :],
-                    out_full_ref[:, columns],
+                    out_full_ref[:, :, columns].reshape(width, 256),
                     preferred_element_type=jnp.float32,
                 ).astype(jnp.bfloat16)
                 return carry
@@ -157,12 +354,17 @@
                     [pair * ones for pair in pairs for ones in (front_ones, back_ones)], axis=0
                 )
                 probs = probs_ref[micro, head, :, rows, :span].reshape(groups * half_rows, span)
-                d_probs = jnp.dot(
-                    d_rows, values_ref[micro, head, :, :span], preferred_element_type=jnp.float32
+                d_probs = lax.dot_general(
+                    d_rows,
+                    values_ref[micro, head, :span, :],
+                    last_dims,
+                    preferred_element_type=jnp.float32,
                 )
                 probs_f = probs.astype(jnp.float32)
                 row_inner = jnp.sum(probs_f * d_probs, axis=-1, keepdims=True)
-                d_scores = (probs_f * (d_probs - row_inner)).astype(jnp.bfloat16)
+                d_scores = (probs_f * (d_probs - row_inner) * (1.0 / math.sqrt(HD))).astype(
+                    jnp.bfloat16
+                )
                 d_query = jnp.dot(
                     d_scores, keys_ref[micro, head, :span, :], preferred_element_type=jnp.float32
                 )
@@ -236,6 +438,8 @@
         return carry
 
     lax.fori_loop(0, micro_count, one_micro, 0)
+    gather_sent(0)
+    gather_sent(1)
     keep = pltpu.make_async_copy(held, upstream_ref, local_sem)
     keep.start()
     keep.wait()
@@ -247,47 +451,62 @@
                 hop(micro, half).wait_send()
 
 
-def chain(cotangent, out_full, in_full, probs, keys, values, queries, inputs, scale, gain, table):
+def chain(cotangent, out_shard, in_shard, queries, keys, values, inputs, gain, table):
     micro_count, length, width = inputs.shape
     half_rows = length // 2
     qd = HEADS * HD
-    qkv_width = in_full.shape[1]
+    groups = HEADS // KVH
+    qkv_width, shard = in_shard.shape
+    shards = width // shard
+    places = shards // 2
     vmem = pl.BlockSpec(memory_space=pltpu.VMEM)
     hbm = pl.BlockSpec(memory_space=pl.ANY)
+    head_rows = pltpu.VMEM((micro_count, KVH, length, 2 * HD), jnp.bfloat16)
+    sums = pltpu.VMEM((KVH, half_rows, 2 * HD), jnp.float32)
+    gather_sem = pltpu.SemaphoreType.DMA((2, places))
+    wide = jax.ShapeDtypeStruct((micro_count, length, width), jnp.bfloat16)
     return pl.pallas_call(
         chain_kernel,
         out_shape=(
-            jax.ShapeDtypeStruct((micro_count, length, width), jnp.bfloat16),
+            wide,
             jax.ShapeDtypeStruct((micro_count, length, qkv_width), jnp.bfloat16),
-            jax.ShapeDtypeStruct((micro_count, length, width), jnp.bfloat16),
+            wide,
+            jax.ShapeDtypeStruct((micro_count, length, qd), jnp.bfloat16),
+            wide,
         ),
-        in_specs=[hbm] + [vmem] * 10,
-        out_specs=(vmem, vmem, hbm),
+        in_specs=[hbm] + [vmem] * 8,
+        out_specs=(vmem, vmem, vmem, vmem, hbm),
         scratch_shapes=[
+            pltpu.VMEM((shards, shard, qd), jnp.bfloat16),
+            pltpu.VMEM((shards, qkv_width, shard), jnp.bfloat16),
+            pltpu.VMEM((micro_count, KVH, groups, length, length), jnp.bfloat16),
+            head_rows,
+            head_rows,
+            pltpu.VMEM((micro_count, KVH, groups, length, 2 * HD), jnp.bfloat16),
+            pltpu.VMEM((micro_count, length, 1), jnp.float32),
             pltpu.VMEM((micro_count, length, width), jnp.bfloat16),
             pltpu.VMEM((half_rows, qd), jnp.bfloat16),
             pltpu.VMEM((half_rows, width), jnp.float32),
-            pltpu.VMEM((KVH, half_rows, 2 * HD), jnp.float32),
-            pltpu.VMEM((KVH, half_rows, 2 * HD), jnp.float32),
+            sums,
+            sums,
             pltpu.SemaphoreType.DMA((micro_count, 2)),
             pltpu.SemaphoreType.DMA((micro_count, 2)),
             pltpu.SemaphoreType.DMA,
+            gather_sem,
+            gather_sem,
+            gather_sem,
+            gather_sem,
+            gather_sem,
         ],
         compiler_params=pltpu.CompilerParams(
-            collective_id=0, has_side_effects=True, vmem_limit_bytes=52 * 2**20
+            collective_id=0, has_side_effects=True, vmem_limit_bytes=56 * 2**20
         ),
         cost_estimate=pl.CostEstimate(
             flops=2 * micro_count * length * width * (qkv_width + qd),
             bytes_accessed=24 * 2**20,
             transcendentals=0,
         ),
-    )(cotangent, out_full, in_full, probs, keys, values, queries, inputs, scale, gain, table)
-
-
-def with_swapped(rows):
-    half_size = HD // 2
-    swapped = jnp.concatenate([rows[..., half_size:], rows[..., :half_size]], axis=-1)
-    return jnp.concatenate([rows, swapped], axis=-1)
+    )(cotangent, out_shard, in_shard, queries, keys, values, inputs, gain, table)
 
 
 def reduce_kernel(
@@ -572,37 +791,21 @@
     queries = saved_queries[0]
     keys_all = saved_keys[0]
     values_all = saved_values[0]
-    gain_row = norm_gain[0]
     micro_count = inputs.shape[0]
     length = inputs.shape[1]
     width = inputs.shape[2]
-    groups = HEADS // KVH
-    out_full = lax.all_gather(output_weight[0], "fsdp", axis=0, tiled=True)
     in_shard = jnp.concatenate([query_weight[0], key_weight[0], value_weight[0]], axis=1)
-    in_full = lax.all_gather(in_shard.T, "fsdp", axis=0, tiled=False)
     qkv_width = in_shard.shape[1]
-    forward_all = jax.vmap(forward_parts, in_axes=(0, 0, 0, 0, None))
-    attn_probs, normed, attn_out = forward_all(inputs, queries, keys_all, values_all, gain_row)
-    scale_inv = norm_parts(inputs)[1]
     cosine, sine = rotary_tables(length, HD)
     table = jnp.concatenate([cosine, cosine, sine, -sine], axis=1)
-    query_grid = with_swapped(
-        queries.reshape(micro_count, length, KVH, groups, HD).transpose(0, 2, 3, 1, 4)
-    )
-    key_grid = with_swapped(keys_all.reshape(micro_count, length, KVH, HD).transpose(0, 2, 1, 3))
-    value_grid = values_all.reshape(micro_count, length, KVH, HD).transpose(0, 2, 3, 1)
-    value_grid = value_grid * jnp.bfloat16(1.0 / math.sqrt(HD))
-    value_grid = jnp.concatenate([value_grid, value_grid], axis=2)
-    grads, qkv_all, upstream_all = chain(
+    grads, qkv_all, normed, attn_out, upstream_all = chain(
         cotangent,
-        out_full,
-        in_full,
-        attn_probs,
-        key_grid,
-        value_grid,
-        query_grid,
+        output_weight[0],
+        in_shard.T,
+        queries,
+        keys_all,
+        values_all,
         inputs,
-        scale_inv,
         norm_gain,
         table,
     )

time: 352 us -> 315 us (0.89)
  Pallas kernels: 215 us -> 303 us
  waiting for transfers between devices: 71.9 us -> 0 us
  local copies, waits for them, and re-layouts: 28 us -> 8.06 us
  between operations: 14.3 us -> 0.73 us
  other arithmetic: 14.3 us -> 2.27 us
  matrix products: 8.26 us -> 0 us
    pallas_call x1, Pallas kernels: 113 us -> 202 us  [chain(): pl.pallas_call(chain_kernel, out_shape=(wide, jax.ShapeDtypeStruct((micro...]
    all_gather x2 -> x0, waiting for transfers between devices: 71.2 us -> none  [the longest x1 38.8 us: on_device(): out_full = lax.all_gather(output_weight[0], 'fsdp', axis=0, tiled=True)]
    all_gather x1 -> x0, local copies, waits for them, and re-layouts: 8.68 us -> none  [on_device(): in_full = lax.all_gather(in_shard.T, 'fsdp', axis=0, tiled=False)]
    sub x1 -> x0, matrix products: 6.88 us -> none  [forward_parts(): weights = jnp.exp(scores - row_peak)]
    convert_element_type x3 -> x0, other arithmetic: 6.09 us -> none  [the longest x1 4.18 us: forward_parts(): (weights / jnp.sum(weights, axis=-1, keepdims=True)).astype(jnp.bfloat16)]
    concatenate x3 -> x0, other arithmetic: 3.79 us -> none  [the longest x2 3.75 us: with_swapped(): return jnp.concatenate([rows, swapped], axis=-1)]
    unnamed x25 -> x12, local copies, waits for them, and re-layouts: 7.64 us -> 3.99 us
    reshape x2 -> x0, local copies, waits for them, and re-layouts: 3.62 us -> none  [on_device(): attn_flat = attn_out.reshape(micro_count * length, -1)]
  transfers between devices with their start and end apart: 2 -> 0, of which waited for: 2 -> 0; matrix products, arithmetic and copies ran while one was open for 11% -> 0% of each run, Pallas kernels for 0% -> 0%
where the time goes in v3:
time: 315 us; the launch traced here: 314 us
  Pallas kernels  303 us (96%)
  local copies, waits for them, and re-layouts  8.06 us (3%)
    pallas_call x1, Pallas kernels, chain(): pl.pallas_call(chain_kernel, out_shape=(wide, jax.ShapeDtypeStruct((micro...  202 us
    pallas_call x1, Pallas kernels, weight_grads(): pl.pallas_call(reduce_kernel, out_shape=jax.ShapeDtypeStruct((shard, colu...  102 us

profile of v3, /device:TPU:0, one launch (start us, length us, event | category | flops | bytes accessed | tf_op | source)
XLA Modules:
  0.0 314.4 jit_solution(5181923054790369186)
XLA Ops:
  0.6 0.0 copy-start.2
  0.6 0.0 copy-start.3
  0.7 0.5 fusion.1
  1.2 0.8 pad_maximum_fusion.table_ref
  2.0 1.2 copy.18
  3.3 0.0 copy-done.2
  3.3 0.1 copy.19
  3.4 0.0 copy-done.3
  3.4 0.1 copy.20
  3.5 0.9 maximum_bitcast_fusion.in_shard_ref
  4.4 201.5 %shard_map.137 = (bf16[2,256,2048]{2,1,0:T(8,128)(2,1)}, bf16[2,256,1536]{2,1,0:T(8,128)(2,1)}, bf16[2,256,2048]{2,1,0:T(8,128)(2,1)}, bf16[2,256,1024]{2,1,0:T(8,128)(2,1)}, bf16[2,256,2048]{2,1,0:T(8,128)(2,1)}) custom-call(bf16[2,256,2048]{2,1,0:T(8,128)(2,1)} %cotangent_ref.1, bf16[256,1024]{1,0:T(8,128)(2,1)} %bitcast.30, ...), custom_call_target="tpu_custom_call" | custom-call | flops 5368709120 | bytes 25165824 | tf_op jit(solution)/shard_map/pallas_call | solution.py:468
  205.9 0.0 copy-start
  205.9 1.2 copy-done
  207.2 101.8 %shard_map.138 = bf16[256,2560]{1,0:T(8,128)(2,1)} custom-call(bf16[512,2048]{1,0:T(8,128)(2,1)} %bitcast.33, bf16[512,1536]{1,0:T(8,128)(2,1)} %bitcast.35, bf16[512,2048]{1,0:T(8,128)(2,1)} %bitcast.34, bf16[512,1024]{1,0:T(8,128)(2,1)S(1)} %bitcast.23), custom_call_target="tpu_custom_call" | custom-call | flops 5368709120 | bytes 8388608 | tf_op jit(solution)/shard_map/pallas_call | solution.py:752
  309.0 0.0 copy-start.1
  309.0 2.4 slice_bitcast_fusion
  311.3 1.7 slice_bitcast_fusion.2
  313.0 0.0 copy-done.1
  313.0 1.3 copy.23
  (1 shorter events, 0.0 us)
Async XLA Ops:
  0.6 2.6 copy-start.2
  0.6 2.7 copy-start.3
  205.9 1.2 copy-start
  309.0 4.1 %copy-start.1 = (bf16[2,256,2048]{2,1,0:T(8,128)(2,1)S(1)}, bf16[2,256,2048]{2,1,0:T(8,128)(2,1)}, u32[]{:S(2)}) copy-start(bf16[2,256,2048]{2,1,0:T(8,128)(2,1)} %get-tuple-element.10) | copy-start | bytes 6291460

commit v4 on v3

--- a/solution.py
+++ b/solution.py
@@ -286,26 +286,6 @@
 
         lax.fori_loop(0, KVH // 2, head_pair, 0)
 
-    gather_first(0)
-
-    @pl.when(is_last)
-    def _():
-        own = pltpu.make_async_copy(cotangent_ref, held, local_sem)
-        own.start()
-        own.wait()
-
-    for step in range(1, places):
-        if step <= micro_count:
-            forward(step - 1)
-        gather_step(0, step)
-    for micro in range(max(places - 1, 0), micro_count):
-        forward(micro)
-    gather_first(1)
-    gather_end(0)
-    for step in range(1, places):
-        gather_step(1, step)
-    gather_end(1)
-
     def hop(micro, half):
         rows = pl.ds(half * half_rows, half_rows)
         return pltpu.make_async_remote_copy(
@@ -324,117 +304,157 @@
     def both_halves(block):
         return block + pltpu.roll(block, HD, 1)
 
+    def attend(micro, half):
+        rows = pl.ds(half * half_rows, half_rows)
+        span = (half + 1) * half_rows
+
+        def attn_tile(tile, carry):
+            columns = pl.ds(pl.multiple_of(tile * 256, 256), 256)
+            d_attn[:, columns] = jnp.dot(
+                held[micro, rows, :],
+                out_full_ref[:, :, columns].reshape(width, 256),
+                preferred_element_type=jnp.float32,
+            ).astype(jnp.bfloat16)
+            return carry
+
+        lax.fori_loop(0, qd // 256, attn_tile, 0)
+        table = table_ref[rows, :]
+        kept = []
+        for head in range(KVH):
+            pairs = [
+                d_attn[:, (head * groups + 2 * i) * HD : (head * groups + 2 * i + 2) * HD]
+                for i in range(groups // 2)
+            ]
+            d_rows = jnp.concatenate(
+                [pair * ones for pair in pairs for ones in (front_ones, back_ones)], axis=0
+            )
+            probs = probs_ref[micro, head, :, rows, :span].reshape(groups * half_rows, span)
+            d_probs = lax.dot_general(
+                d_rows,
+                values_ref[micro, head, :span, :],
+                last_dims,
+                preferred_element_type=jnp.float32,
+            )
+            probs_f = probs.astype(jnp.float32)
+            row_inner = jnp.sum(probs_f * d_probs, axis=-1, keepdims=True)
+            d_scores = (probs_f * (d_probs - row_inner) * (1.0 / math.sqrt(HD))).astype(
+                jnp.bfloat16
+            )
+            d_query = jnp.dot(
+                d_scores, keys_ref[micro, head, :span, :], preferred_element_type=jnp.float32
+            )
+            turned = [
+                both_halves(d_query[g * half_rows : (g + 1) * half_rows] * table)
+                for g in range(groups)
+            ]
+            for i in range(groups // 2):
+                start = (head * groups + 2 * i) * HD
+                qkv_ref[micro, rows, start : start + 2 * HD] = jnp.where(
+                    front, turned[2 * i], turned[2 * i + 1]
+                ).astype(jnp.bfloat16)
+            query_rows = queries_ref[micro, head, :, rows, :].reshape(
+                groups * half_rows, 2 * HD
+            )
+            across = (((0,), (0,)), ((), ()))
+            d_key = lax.dot_general(
+                d_scores, query_rows, across, preferred_element_type=jnp.float32
+            )
+            d_value = lax.dot_general(
+                probs, d_rows, across, preferred_element_type=jnp.float32
+            )
+            if half == 1:
+                key_sums[head] = d_key[:half_rows]
+                value_sums[head] = d_value[:half_rows]
+                d_key = d_key[half_rows:]
+                d_value = d_value[half_rows:]
+            else:
+                d_key = d_key + key_sums[head]
+                d_value = d_value + value_sums[head]
+            kept.append((both_halves(d_key * table), both_halves(d_value)))
+            if head % 2 == 1:
+                start = qd + (head - 1) * HD
+                for which in range(2):
+                    at = start + which * kvd
+                    qkv_ref[micro, rows, at : at + 2 * HD] = jnp.where(
+                        front, kept[head - 1][which], kept[head][which]
+                    ).astype(jnp.bfloat16)
+
+    def project(micro, half):
+        rows = pl.ds(half * half_rows, half_rows)
+        scale = scale_ref[micro, rows, :]
+
+        def normed_tile(tile, inner):
+            columns = pl.ds(pl.multiple_of(tile * shard, shard), shard)
+            d_normed = jnp.dot(
+                qkv_ref[micro, rows, :], in_full_ref[tile], preferred_element_type=jnp.float32
+            )
+            scaled = d_normed * gain_ref[:, columns].astype(jnp.float32)
+            scaled_rows[:, columns] = scaled
+            unit = inputs_ref[micro, rows, columns].astype(jnp.float32) * scale
+            return inner + jnp.sum(scaled * unit, axis=-1, keepdims=True)
+
+        inner = lax.fori_loop(
+            0, shards, normed_tile, jnp.zeros((half_rows, 1), jnp.float32)
+        ) * (1.0 / width)
+
+        def grad_tile(tile, carry):
+            columns = pl.ds(pl.multiple_of(tile * shard, shard), shard)
+            unit = inputs_ref[micro, rows, columns].astype(jnp.float32) * scale
+            d_inputs = scale * (scaled_rows[:, columns] - unit * inner)
+            grad_ref[micro, rows, columns] = (
+                held[micro, rows, columns].astype(jnp.float32) + d_inputs
+            ).astype(jnp.bfloat16)
+            return carry
+
+        lax.fori_loop(0, shards, grad_tile, 0)
+
+        @pl.when(section > 0)
+        def _():
+            hop(micro, half).start()
+
+    gather_first(0)
+
+    @pl.when(is_last)
+    def _():
+        own = pltpu.make_async_copy(cotangent_ref, held, local_sem)
+        own.start()
+        own.wait()
+
+    for step in range(1, places):
+        if step <= micro_count:
+            forward(step - 1)
+        gather_step(0, step)
+    for micro in range(max(places - 1, 0), micro_count):
+        forward(micro)
+    gather_first(1)
+    gather_end(0)
+    for step in range(1, places):
+        if step <= micro_count:
+
+            @pl.when(is_last)
+            def _():
+                attend(step - 1, 1)
+                attend(step - 1, 0)
+
+        gather_step(1, step)
+    for micro in range(max(places - 1, 0), micro_count):
+
+        @pl.when(is_last)
+        def _():
+            attend(micro, 1)
+            attend(micro, 0)
+
+    gather_end(1)
+
     def one_micro(micro, carry):
         for half in (1, 0):
-            rows = pl.ds(half * half_rows, half_rows)
-            span = (half + 1) * half_rows
 
             @pl.when(section < sections - 1)
             def _():
                 hop(micro, half).wait_recv()
-
-            def attn_tile(tile, carry):
-                columns = pl.ds(pl.multiple_of(tile * 256, 256), 256)
-                d_attn[:, columns] = jnp.dot(
-                    held[micro, rows, :],
-                    out_full_ref[:, :, columns].reshape(width, 256),
-                    preferred_element_type=jnp.float32,
-                ).astype(jnp.bfloat16)
-                return carry
-
-            lax.fori_loop(0, qd // 256, attn_tile, 0)
-            table = table_ref[rows, :]
-            kept = []
-            for head in range(KVH):
-                pairs = [
-                    d_attn[:, (head * groups + 2 * i) * HD : (head * groups + 2 * i + 2) * HD]
-                    for i in range(groups // 2)
-                ]
-                d_rows = jnp.concatenate(
-                    [pair * ones for pair in pairs for ones in (front_ones, back_ones)], axis=0
-                )
-                probs = probs_ref[micro, head, :, rows, :span].reshape(groups * half_rows, span)
-                d_probs = lax.dot_general(
-                    d_rows,
-                    values_ref[micro, head, :span, :],
-                    last_dims,
-                    preferred_element_type=jnp.float32,
-                )
-                probs_f = probs.astype(jnp.float32)
-                row_inner = jnp.sum(probs_f * d_probs, axis=-1, keepdims=True)
-                d_scores = (probs_f * (d_probs - row_inner) * (1.0 / math.sqrt(HD))).astype(
-                    jnp.bfloat16
-                )
-                d_query = jnp.dot(
-                    d_scores, keys_ref[micro, head, :span, :], preferred_element_type=jnp.float32
-                )
-                turned = [
-                    both_halves(d_query[g * half_rows : (g + 1) * half_rows] * table)
-                    for g in range(groups)
-                ]
-                for i in range(groups // 2):
-                    start = (head * groups + 2 * i) * HD
-                    qkv_ref[micro, rows, start : start + 2 * HD] = jnp.where(
-                        front, turned[2 * i], turned[2 * i + 1]
-                    ).astype(jnp.bfloat16)
-                query_rows = queries_ref[micro, head, :, rows, :].reshape(
-                    groups * half_rows, 2 * HD
-                )
-                across = (((0,), (0,)), ((), ()))
-                d_key = lax.dot_general(
-                    d_scores, query_rows, across, preferred_element_type=jnp.float32
-                )
-                d_value = lax.dot_general(
-                    probs, d_rows, across, preferred_element_type=jnp.float32
-                )
-                if half == 1:
-                    key_sums[head] = d_key[:half_rows]
-                    value_sums[head] = d_value[:half_rows]
-                    d_key = d_key[half_rows:]
-                    d_value = d_value[half_rows:]
-                else:
-                    d_key = d_key + key_sums[head]
-                    d_value = d_value + value_sums[head]
-                kept.append((both_halves(d_key * table), both_halves(d_value)))
-                if head % 2 == 1:
-                    start = qd + (head - 1) * HD
-                    for which in range(2):
-                        at = start + which * kvd
-                        qkv_ref[micro, rows, at : at + 2 * HD] = jnp.where(
-                            front, kept[head - 1][which], kept[head][which]
-                        ).astype(jnp.bfloat16)
-
-            scale = scale_ref[micro, rows, :]
-
-            def normed_tile(tile, inner):
-                columns = pl.ds(pl.multiple_of(tile * shard, shard), shard)
-                d_normed = jnp.dot(
-                    qkv_ref[micro, rows, :], in_full_ref[tile], preferred_element_type=jnp.float32
-                )
-                scaled = d_normed * gain_ref[:, columns].astype(jnp.float32)
-                scaled_rows[:, columns] = scaled
-                unit = inputs_ref[micro, rows, columns].astype(jnp.float32) * scale
-                return inner + jnp.sum(scaled * unit, axis=-1, keepdims=True)
-
-            inner = lax.fori_loop(
-                0, shards, normed_tile, jnp.zeros((half_rows, 1), jnp.float32)
-            ) * (1.0 / width)
-
-            def grad_tile(tile, carry):
-                columns = pl.ds(pl.multiple_of(tile * shard, shard), shard)
-                unit = inputs_ref[micro, rows, columns].astype(jnp.float32) * scale
-                d_inputs = scale * (scaled_rows[:, columns] - unit * inner)
-                grad_ref[micro, rows, columns] = (
-                    held[micro, rows, columns].astype(jnp.float32) + d_inputs
-                ).astype(jnp.bfloat16)
-                return carry
-
-            lax.fori_loop(0, shards, grad_tile, 0)
-
-            @pl.when(section > 0)
-            def _():
-                hop(micro, half).start()
-
+                attend(micro, half)
+
+            project(micro, half)
         return carry
 
     lax.fori_loop(0, micro_count, one_micro, 0)
@@ -514,7 +534,10 @@
     qkv_ref,
     upstream_ref,
     attn_ref,
-    out_ref,
+    query_out,
+    key_out,
+    value_out,
+    output_out,
     for_twin,
     from_twin,
     stage,
@@ -570,14 +593,36 @@
     def to_twin(t):
         return remote(for_twin.at[t], from_twin.at[t], twin_send.at[t], twin_recv.at[t], twin)
 
-    def go_up(t):
-        return remote(stage.at[t], line.at[t], line_send.at[t], line_recv.at[t], upper)
-
-    def go_down(t):
-        return remote(stage.at[t], line.at[t], line_send.at[t], line_recv.at[t], lower)
-
-    def end_down(t):
-        return remote(stage.at[t], other, line_send.at[t], other_recv, lower)
+    part_columns = columns_out // 2
+
+    def part_of(part):
+        return pl.ds(part * part_columns, part_columns)
+
+    def go(t, part, device):
+        columns = part_of(part)
+        return remote(
+            stage.at[t, :, columns],
+            line.at[t, :, columns],
+            line_send.at[t, part],
+            line_recv.at[t, part],
+            device,
+        )
+
+    def go_up(t, part):
+        return go(t, part, upper)
+
+    def go_down(t, part):
+        return go(t, part, lower)
+
+    def end_down(t, part):
+        columns = part_of(part)
+        return remote(
+            stage.at[t, :, columns],
+            other.at[:, columns],
+            line_send.at[t, part],
+            other_recv.at[part],
+            lower,
+        )
 
     across = (((0,), (0,)), ((), ()))
 
@@ -618,7 +663,7 @@
     def target(step):
         return jnp.where(low_half, places - 1 - step, step)
 
-    def send_twin(step, carry):
+    def send_twin(step):
         t = target(step)
 
         def store(columns, block):
@@ -626,11 +671,14 @@
 
         partial(t, 1 - core, store)
         to_twin(t).start()
-        return carry
-
-    lax.fori_loop(0, places, send_twin, 0)
+
+    send_twin(0)
 
     def chip_sum(step, carry):
+        @pl.when(step + 1 < places)
+        def _():
+            send_twin(step + 1)
+
         t = target(step)
         to_twin(t).wait_recv()
 
@@ -643,98 +691,115 @@
 
         @pl.when(jnp.logical_and(place == 0, t > place))
         def _():
-            go_up(t).start()
+            go_up(t, 0).start()
+            go_up(t, 1).start()
 
         @pl.when(jnp.logical_and(place == places - 1, t < place - 1))
         def _():
-            go_down(t).start()
+            go_down(t, 0).start()
+            go_down(t, 1).start()
 
         @pl.when(jnp.logical_and(place == places - 1, t == place - 1))
         def _():
-            end_down(t).start()
+            end_down(t, 0).start()
+            end_down(t, 1).start()
 
         return carry
 
     lax.fori_loop(0, places, chip_sum, 0)
 
-    def add_line(t):
+    def add_line(t, part):
         def tile(tile, carry):
-            columns = pl.ds(pl.multiple_of(tile * 512, 512), 512)
+            columns = pl.ds(
+                pl.multiple_of(part * part_columns + tile * 256, 256), 256
+            )
             stage[t, :, columns] = (
                 stage[t, :, columns].astype(jnp.float32) + line[t, :, columns].astype(jnp.float32)
             ).astype(jnp.bfloat16)
             return carry
 
-        lax.fori_loop(0, columns_out // 512, tile, 0)
+        lax.fori_loop(0, part_columns // 256, tile, 0)
 
     def relay(tick, carry):
-        @pl.when(jnp.logical_and(has_lower, place <= tick))
-        def _():
-            t = places - 1 - tick + place
-            go_up(t).wait_recv()
-            add_line(t)
-            go_up(t).start()
-
-        @pl.when(jnp.logical_and(has_upper, tick >= places - 1 - place))
-        def _():
-            t = tick - (places - 1 - place)
-            go_down(t).wait_recv()
-            add_line(t)
-
-            @pl.when(t < place - 1)
-            def _():
-                go_down(t).start()
-
-            @pl.when(t == place - 1)
-            def _():
-                end_down(t).start()
+        for part in range(2):
+
+            @pl.when(jnp.logical_and(has_lower, place <= tick))
+            def _():
+                t = places - 1 - tick + place
+                go_up(t, part).wait_recv()
+                add_line(t, part)
+                go_up(t, part).start()
+
+            @pl.when(jnp.logical_and(has_upper, tick >= places - 1 - place))
+            def _():
+                t = tick - (places - 1 - place)
+                go_down(t, part).wait_recv()
+                add_line(t, part)
+
+                @pl.when(t < place - 1)
+                def _():
+                    go_down(t, part).start()
+
+                @pl.when(t == place - 1)
+                def _():
+                    end_down(t, part).start()
 
         return carry
 
     lax.fori_loop(0, places - 1, relay, 0)
 
-    @pl.when(has_lower)
-    def _():
-        go_up(place).wait_recv()
-
-    @pl.when(has_upper)
-    def _():
-        end_down(place).wait_recv()
-
-    def finish(tile, carry):
-        columns = pl.ds(pl.multiple_of(tile * 512, 512), 512)
-        total = stage[place, :, columns].astype(jnp.float32)
-
-        @pl.when(jnp.logical_not(has_lower))
-        def _():
-            out_ref[:, columns] = (total + other[:, columns].astype(jnp.float32)).astype(
-                jnp.bfloat16
-            )
-
-        @pl.when(jnp.logical_not(has_upper))
-        def _():
-            out_ref[:, columns] = (total + line[place, :, columns].astype(jnp.float32)).astype(
-                jnp.bfloat16
-            )
-
-        @pl.when(jnp.logical_and(has_lower, has_upper))
-        def _():
-            out_ref[:, columns] = (
-                total
-                + line[place, :, columns].astype(jnp.float32)
-                + other[:, columns].astype(jnp.float32)
-            ).astype(jnp.bfloat16)
-
-        return carry
-
-    lax.fori_loop(0, columns_out // 512, finish, 0)
+    for part in range(2):
+
+        @pl.when(has_lower)
+        def _():
+            go_up(place, part).wait_recv()
+
+        @pl.when(has_upper)
+        def _():
+            end_down(place, part).wait_recv()
+
+    def finish(out_ref, start):
+        def tile(tile, carry):
+            columns = pl.ds(pl.multiple_of(start + tile * 256, 256), 256)
+            own_columns = pl.ds(pl.multiple_of(tile * 256, 256), 256)
+            total = stage[place, :, columns].astype(jnp.float32)
+
+            @pl.when(jnp.logical_not(has_lower))
+            def _():
+                out_ref[:, own_columns] = (
+                    total + other[:, columns].astype(jnp.float32)
+                ).astype(jnp.bfloat16)
+
+            @pl.when(jnp.logical_not(has_upper))
+            def _():
+                out_ref[:, own_columns] = (
+                    total + line[place, :, columns].astype(jnp.float32)
+                ).astype(jnp.bfloat16)
+
+            @pl.when(jnp.logical_and(has_lower, has_upper))
+            def _():
+                out_ref[:, own_columns] = (
+                    total
+                    + line[place, :, columns].astype(jnp.float32)
+                    + other[:, columns].astype(jnp.float32)
+                ).astype(jnp.bfloat16)
+
+            return carry
+
+        lax.fori_loop(0, out_ref.shape[1] // 256, tile, 0)
+
+    start = 0
+    for out_ref in (query_out, key_out, value_out, output_out):
+        finish(out_ref, start)
+        start += out_ref.shape[1]
 
     def sent(t, carry):
         to_twin(t).wait_send()
 
         @pl.when(t != place)
         def _():
-            go_up(t).wait_send()
+            go_up(t, 0).wait_send()
+            go_up(t, 1).wait_send()
 
         return carry
 
@@ -751,9 +816,12 @@
     block = pltpu.VMEM((places, shard, columns), jnp.bfloat16)
     return pl.pallas_call(
         reduce_kernel,
-        out_shape=jax.ShapeDtypeStruct((shard, columns), jnp.bfloat16),
+        out_shape=tuple(
+            jax.ShapeDtypeStruct((shard, size), jnp.bfloat16)
+            for size in (HEADS * HD, KVH * HD, KVH * HD, attn.shape[1])
+        ),
         in_specs=[vmem] * 4,
-        out_specs=vmem,
+        out_specs=(vmem,) * 4,
         scratch_shapes=[
             block,
             block,
@@ -762,9 +830,9 @@
             pltpu.VMEM((shard, columns), jnp.bfloat16),
             pltpu.SemaphoreType.DMA((places,)),
             pltpu.SemaphoreType.DMA((places,)),
-            pltpu.SemaphoreType.DMA((places,)),
-            pltpu.SemaphoreType.DMA((places,)),
-            pltpu.SemaphoreType.DMA,
+            pltpu.SemaphoreType.DMA((places, 2)),
+            pltpu.SemaphoreType.DMA((places, 2)),
+            pltpu.SemaphoreType.DMA((2,)),
         ],
         compiler_params=pltpu.CompilerParams(
             collective_id=1, has_side_effects=True, vmem_limit_bytes=52 * 2**20
@@ -813,13 +881,9 @@
     qkv_flat = qkv_all.reshape(micro_count * length, qkv_width)
     attn_flat = attn_out.reshape(micro_count * length, -1)
     upstream_flat = upstream_all.reshape(micro_count * length, width)
-    summed = weight_grads(normed_flat, qkv_flat, upstream_flat, attn_flat)
-    query_cols = query_weight.shape[2]
-    key_cols = key_weight.shape[2]
-    grad_query = summed[:, :query_cols]
-    grad_key = summed[:, query_cols : query_cols + key_cols]
-    grad_value = summed[:, query_cols + key_cols : qkv_width]
-    grad_output = summed[:, qkv_width:]
+    grad_query, grad_key, grad_value, grad_output = weight_grads(
+        normed_flat, qkv_flat, upstream_flat, attn_flat
+    )
     return (
         grads[None],
         grad_query[None],

time: 315 us -> 302 us (0.959)
  Pallas kernels: 303 us -> 292 us
    pallas_call x1, Pallas kernels: 102 us -> 94.5 us  [weight_grads(): pl.pallas_call(reduce_kernel, out_shape=tuple((jax.ShapeDtypeStruct((shar...]
    broadcast_in_dim x2 -> x0, local copies, waits for them, and re-layouts: 4.07 us -> none  [the longest x1 2.38 us: on_device(): grad_output[None]]
    pallas_call x1, Pallas kernels: 202 us -> 198 us  [chain(): pl.pallas_call(chain_kernel, out_shape=(wide, jax.ShapeDtypeStruct((micro...]
where the time goes in v4:
time: 302 us
  Pallas kernels  292 us (97%)
  local copies, waits for them, and re-layouts  6.57 us (2%)
    pallas_call x1, Pallas kernels, chain(): pl.pallas_call(chain_kernel, out_shape=(wide, jax.ShapeDtypeStruct((micro...  198 us
    pallas_call x1, Pallas kernels, weight_grads(): pl.pallas_call(reduce_kernel, out_shape=tuple((jax.ShapeDtypeStruct((shar...  94.5 us
    unnamed x12, local copies, waits for them, and re-layouts  6.57 us

profile of v4, /device:TPU:0, one launch (start us, length us, event | category | flops | bytes accessed | tf_op | source)
XLA Modules:
  0.0 301.9 jit_solution(10893328324343178793)
XLA Ops:
  0.6 0.0 copy-start.1
  0.7 0.5 fusion.1
  1.2 0.8 pad_maximum_fusion.table_ref
  2.0 1.2 copy.18
  3.2 1.0 copy.19
  4.3 0.0 copy-done.1
  4.3 0.1 copy.20
  4.4 0.9 maximum_bitcast_fusion.in_shard_ref
  5.3 197.9 %shard_map.137 = (bf16[2,256,2048]{2,1,0:T(8,128)(2,1)}, bf16[2,256,1536]{2,1,0:T(8,128)(2,1)}, bf16[2,256,2048]{2,1,0:T(8,128)(2,1)}, bf16[2,256,1024]{2,1,0:T(8,128)(2,1)}, bf16[2,256,2048]{2,1,0:T(8,128)(2,1)}) custom-call(bf16[2,256,2048]{2,1,0:T(8,128)(2,1)} %cotangent_ref.1, bf16[256,1024]{1,0:T(8,128)(2,1)} %bitcast.29, ...), custom_call_target="tpu_custom_call" | custom-call | flops 5368709120 | bytes 25165824 | tf_op jit(solution)/shard_map/pallas_call | solution.py:488
  203.2 0.0 copy-start
  203.2 94.5 %shard_map.138 = (bf16[256,1024]{1,0:T(8,128)(2,1)S(1)}, bf16[256,256]{1,0:T(8,128)(2,1)S(1)}, bf16[256,256]{1,0:T(8,128)(2,1)S(1)}, bf16[256,1024]{1,0:T(8,128)(2,1)S(1)}) custom-call(bf16[512,2048]{1,0:T(8,128)(2,1)} %bitcast.32, bf16[512,1536]{1,0:T(8,128)(2,1)} %bitcast.34, bf16[512,2048]{1,0:T(8,128)(2,1)} %bitcast.33, bf16[512,1024]{1,0:T(8,128)(2,1)} %bitcast.35), custom_call_target="tpu_custom_call" | custom-call | flops 5368709120 | bytes 8388608 | tf_op jit(solution)/shard_map/pallas_call | solution.py:817
  297.7 0.0 copy-done
  297.7 1.3 copy.27
  299.0 0.8 copy.28
  299.8 0.7 copy.29
  300.5 0.7 copy.30
  301.1 0.8 copy.31
  (1 shorter events, 0.0 us)
Async XLA Ops:
  0.6 3.6 %copy-start.1 = (bf16[1,256,256]{2,1,0:T(8,128)(2,1)S(1)}, bf16[1,256,256]{2,1,0:T(8,128)(2,1)}, u32[]{:S(2)}) copy-start(bf16[1,256,256]{2,1,0:T(8,128)(2,1)} %param.18) | copy-start | bytes 393220
  203.2 94.5 %copy-start = (bf16[2,256,2048]{2,1,0:T(8,128)(2,1)S(1)}, bf16[2,256,2048]{2,1,0:T(8,128)(2,1)}, u32[]{:S(2)}) copy-start(bf16[2,256,2048]{2,1,0:T(8,128)(2,1)} %get-tuple-element.14) | copy-start | bytes 6291460
